TPU v7x, 256 devices: a whole 4x4x8 slice. The times are simulated.
256 devices in a mesh: sector: 16 (over y, x), box: 16 (over z, core).
Axes of the slice: x: 4, y: 4, z: 8, core: 2. Of those that a mesh axis runs over, the one named last changes fastest.
Arguments:
- positions: float32 [3, 16, 1024, 128], P(None, 'sector', 'box'), may hold values from -0.9 to 0.9
- strengths: float32 [3, 16, 1024, 128], P(None, 'sector', 'box'), may hold values from -6 to 6
- counts: int32 [16, 1024], P('sector', 'box'), may hold values from 1 to 128
- cross_slot: int32 [16, 4096], P('sector', 'box'), may hold values from 0 to 8191, as said below
- arrive_box: int32 [16, 4096], P('sector', 'box'), may hold values from 0 to 63
- il_source: int32 [16, 1024, 16], P('sector', 'box'), may hold values from 0 to 63
- il_class: int32 [16, 1024, 16], P('sector', 'box'), may hold values from 0 to 3
- m2m: bfloat16 [4, 441, 441], replicated, may hold values from -0.125 to 0.125
- m2l_leaf: bfloat16 [4, 441, 441], replicated, may hold values from -0.0625 to 0.0625
- tree_up: bfloat16 [2, 441, 441], replicated, may hold values from -0.21875 to 0.21875
- tree_m2l: bfloat16 [2, 441, 441], replicated, may hold values from -0.25 to 0.25
- m2l_sector: bfloat16 [15, 441, 441], replicated, may hold values from -0.078125 to 0.078125
Outputs:
- new_positions: float32 [3, 16, 1024, 128], P(None, 'sector', 'box')
- velocity: float32 [3, 16, 1024, 128], P(None, 'sector', 'box')
Inputs may be any that keep to these rules, and one draw needn't show every extreme that they name: `cross_slot`: within one block's 256 entries the slot numbers are distinct; a slot beyond its box's count carries nothing.
All inputs are finite; a program needn't handle non-finite values.
Results may differ from a plain program's by a relative error of at most 0.006.
Values may be sent and summed in bfloat16 or wider, within the bound.
A program may use at most 128 MiB of HBM per device.

v0:
```python
import math

import jax
import jax.numpy as jnp
from jax import lax
from jax.sharding import PartitionSpec as P

TERMS = 21
LEVELS_DEV = 3
NCLASS = 4


DELTA_SQ = 0.25
TIME_STEP = 0.02
INV_FOUR_PI = 1.0 / (4.0 * math.pi)
HIGHEST_PRECISION = lax.Precision.HIGHEST
OFFSETS = ((0.0, 0.0, 0.0), (0.0, 0.0, -2.0), (0.0, 0.0, 2.0), (-2.0, 0.0, 0.0), (2.0, 0.0, 0.0))


def with_halo(array, sides, width, wrap):
    for axis, dim in sides:
        devices, length = (lax.axis_size(axis), array.shape[dim])
        up = [(i, (i + 1) % devices) for i in range(devices if wrap else devices - 1)]
        down = [(j, i) for i, j in up]
        last = lax.slice_in_dim(array, length - width, length, axis=dim)
        first = lax.slice_in_dim(array, 0, width, axis=dim)
        before = lax.ppermute(last, axis, up)
        after = lax.ppermute(first, axis, down)
        array = jnp.concatenate([before, array, after], axis=dim)
    return array


def partner_2(block, axis, distance):
    count = lax.axis_size(axis)
    route = []
    for low in range(count):
        high = low | 1 << distance
        if high != low and high < count:
            route += [(low, high), (high, low)]
    return lax.ppermute(block, axis, route)


def passed_along(array, axis, by):
    devices = lax.axis_size(axis)
    return lax.ppermute(array, axis, [(i, (i + by) % devices) for i in range(devices)])


def chebyshev(coordinate):
    scaled = 0.5 * coordinate
    series = [jnp.ones_like(scaled), scaled]
    for order in range(2, TERMS):
        series.append(2.0 * scaled * series[-1] - series[-2])
    return jnp.stack(series[:TERMS])


def multipoles(cheb_a, cheb_b, weights):
    weighted = weights[:, None] * cheb_a[None]
    return jnp.einsum("cjnp,knp->ncjk", weighted, cheb_b, precision=HIGHEST_PRECISION)


def evaluate(local, cheb_a, cheb_b):
    shaped = local.reshape(local.shape[0], 3, TERMS, TERMS)
    partial_sum = jnp.einsum("ncjk,knp->cjnp", shaped, cheb_b, precision=HIGHEST_PRECISION)
    return jnp.sum(partial_sum * cheb_a[None], axis=1) / TERMS


def pair_velocity(target, source, weight, offset):
    delta_x = target[0][:, :, None] - (source[0][:, None, :] + offset[0])
    delta_y = target[1][:, :, None] - (source[1][:, None, :] + offset[1])
    delta_z = target[2][:, :, None] - (source[2][:, None, :] + offset[2])
    radius_sq = delta_x * delta_x + delta_y * delta_y + delta_z * delta_z + DELTA_SQ
    inverse = INV_FOUR_PI / (radius_sq * jnp.sqrt(radius_sq))
    weight_x = weight[0][:, None, :]
    weight_y = weight[1][:, None, :]
    weight_z = weight[2][:, None, :]
    speed_x = jnp.sum(inverse * (weight_y * delta_z - weight_z * delta_y), axis=2)
    speed_y = jnp.sum(inverse * (weight_z * delta_x - weight_x * delta_z), axis=2)
    speed_z = jnp.sum(inverse * (weight_x * delta_y - weight_y * delta_x), axis=2)
    return jnp.stack([speed_x, speed_y, speed_z])


def near_field(places, weights):
    box_count, slots = (places.shape[1], places.shape[2])
    stacked = jnp.concatenate([places, weights], axis=0)[:, None]
    beside = with_halo(stacked.astype(jnp.bfloat16), (("sector", 1),), 1, True).astype(
        stacked.dtype
    )
    along = with_halo(stacked.astype(jnp.bfloat16), (("box", 2),), 1, False).astype(stacked.dtype)
    sources = [stacked[:, 0], along[:, 0, :box_count], along[:, 0, 2:], beside[:, 0], beside[:, 2]]
    block = math.gcd(box_count, 64)
    block_count = box_count // block

    def arrange(array):
        return array.reshape(array.shape[0], block_count, block, slots).transpose(1, 0, 2, 3)

    inputs = (arrange(places),) + tuple((arrange(item) for item in sources))

    def block_velocity(items):
        summed = jnp.zeros_like(items[0])
        for index in range(5):
            summed = summed + pair_velocity(
                items[0], items[1 + index][:3], items[1 + index][3:], OFFSETS[index]
            )
        return summed

    result = lax.map(block_velocity, inputs)
    return result.transpose(1, 0, 2, 3).reshape(3, box_count, slots)


def merge_pair(current, partner, side_bit, tree_up):
    lower_node = jnp.where(side_bit == 0, current, partner)
    upper_node = jnp.where(side_bit == 0, partner, current)
    merged = jnp.dot(lower_node, tree_up[0], preferred_element_type=jnp.float32) + jnp.dot(
        upper_node, tree_up[1], preferred_element_type=jnp.float32
    )
    return merged.astype(jnp.bfloat16)


def far_field(
    places,
    weights,
    arrival_terms,
    il_source,
    il_class,
    m2m,
    m2l_leaf,
    tree_up,
    tree_m2l,
    m2l_sector,
):
    box_count = places.shape[1]
    coef = TERMS * TERMS
    cheb_a = chebyshev(places[0])
    cheb_b = chebyshev(places[1])
    leaf = (
        (multipoles(cheb_a, cheb_b, weights) + arrival_terms)
        .reshape(box_count, 3, coef)
        .astype(jnp.bfloat16)
    )
    upward = leaf
    for depth in range(LEVELS_DEV):
        grouped = upward.reshape(-1, 4, 3, coef)
        upward = jnp.einsum(
            "gocx,oxy->gcy", grouped, m2m, preferred_element_type=jnp.float32
        ).astype(jnp.bfloat16)
    block_root = upward[0]
    box_index = lax.axis_index("box")
    depth_count = lax.axis_size("box").bit_length() - 1
    siblings = []
    side_bits = []
    current = block_root
    for depth in range(depth_count):
        partner = partner_2(current, "box", depth)
        side_bit = box_index >> depth & 1
        siblings.append(partner)
        side_bits.append(side_bit)
        current = merge_pair(current, partner, side_bit, tree_up)
    sector_index = lax.axis_index("sector")
    sector_count = lax.axis_size("sector")
    piece = lax.all_gather(current[None], "sector", axis=0, tiled=True)
    source_ids = jnp.arange(piece.shape[0], dtype=jnp.int32)
    distance = (source_ids - sector_index) % sector_count
    matrices = m2l_sector[jnp.maximum(distance - 1, 0)]
    masked_piece = jnp.where((distance != 0)[:, None, None], piece, jnp.zeros_like(piece))
    far_sum = jnp.einsum("ncx,nxy->cy", masked_piece, matrices, preferred_element_type=jnp.float32)
    local = far_sum.astype(jnp.bfloat16)
    for depth in reversed(range(depth_count)):
        up_side = lax.dynamic_index_in_dim(tree_up, side_bits[depth], 0, keepdims=False)
        cross_side = lax.dynamic_index_in_dim(tree_m2l, side_bits[depth], 0, keepdims=False)
        downward = jnp.einsum(
            "cy,xy->cx", local, up_side, preferred_element_type=jnp.float32
        ) + jnp.dot(siblings[depth], cross_side, preferred_element_type=jnp.float32)
        local = downward.astype(jnp.bfloat16)
    parent_local = local[None]
    child = jnp.zeros((box_count, 3, coef), jnp.float32)
    for depth in range(LEVELS_DEV):
        child = jnp.einsum(
            "gcy,oxy->gocx", parent_local, m2m, preferred_element_type=jnp.float32
        ).reshape(-1, 3, coef)
        if depth + 1 < LEVELS_DEV:
            parent_local = child.astype(jnp.bfloat16)
    box_ids = jnp.arange(box_count, dtype=jnp.int32)
    source_hit = (il_source[0][:, :, None] == box_ids[None, None, :]).astype(jnp.bfloat16)
    class_hit = (
        il_class[0][:, :, None] == jnp.arange(NCLASS, dtype=jnp.int32)[None, None, :]
    ).astype(jnp.bfloat16)
    pair_counts = jnp.einsum(
        "bic,bis->cbs", class_hit, source_hit, preferred_element_type=jnp.float32
    ).astype(jnp.bfloat16)
    presum = jnp.einsum(
        "cbs,sx->cbx",
        pair_counts,
        leaf.reshape(box_count, 3 * coef),
        preferred_element_type=jnp.float32,
    )
    presum = presum.astype(jnp.bfloat16).reshape(NCLASS, box_count * 3, coef)
    translated = jnp.einsum(
        "cnx,cxy->ny", presum, m2l_leaf, preferred_element_type=jnp.float32
    ).reshape(box_count, 3, coef)
    return evaluate(child + translated, cheb_a, cheb_b)


def per_device(
    positions,
    strengths,
    counts,
    cross_slot,
    arrive_box,
    il_source,
    il_class,
    m2m,
    m2l_leaf,
    tree_up,
    tree_m2l,
    m2l_sector,
):
    box_count, slots = (positions.shape[2], positions.shape[3])
    slot_ids = jnp.arange(slots, dtype=jnp.int32)
    present = (slot_ids[None, :] < counts[0][:, None]).astype(jnp.float32)
    crossing = cross_slot[0]
    departed = jnp.zeros((box_count * slots,), jnp.float32).at[crossing].set(1.0)
    live = present * (1.0 - departed.reshape(box_count, slots))
    flat_places = positions[:, 0].reshape(3, box_count * slots)
    flat_strength = strengths[:, 0].reshape(3, box_count * slots)
    leave_present = present.reshape(-1)[crossing]
    leaving = jnp.concatenate(
        [flat_places[:, crossing], flat_strength[:, crossing] * leave_present[None]], axis=0
    )
    arrived = passed_along(leaving, "sector", 1)
    arrive_cheb_a = chebyshev(arrived[0][:, None])
    arrive_cheb_b = chebyshev(arrived[1][:, None])
    arrival_each = multipoles(arrive_cheb_a, arrive_cheb_b, arrived[3:6][:, :, None])
    box_ids = jnp.arange(box_count, dtype=jnp.int32)
    landing = (arrive_box[0][None, :] == box_ids[:, None]).astype(jnp.float32)
    arrival_terms = jnp.dot(
        landing, arrival_each.reshape(landing.shape[1], -1), precision=HIGHEST_PRECISION
    )
    arrival_terms = arrival_terms.reshape(box_count, 3, TERMS, TERMS)
    places = positions[:, 0]
    weights = strengths[:, 0] * live[None]
    velocity = jnp.zeros_like(places)
    for substep in range(2):
        near = near_field(places, weights)
        far = far_field(
            places,
            weights,
            arrival_terms,
            il_source,
            il_class,
            m2m,
            m2l_leaf,
            tree_up,
            tree_m2l,
            m2l_sector,
        )
        velocity = near + far
        places = places + TIME_STEP * velocity
    return (places[:, None], velocity[:, None])


def solution(mesh):
    placed = (
        P(None, "sector", "box", None),
        P(None, "sector", "box", None),
        P("sector", "box"),
        P("sector", "box"),
        P("sector", "box"),
        P("sector", "box", None),
        P("sector", "box", None),
        P(),
        P(),
        P(),
        P(),
        P(),
    )
    return jax.shard_map(
        per_device,
        mesh=mesh,
        in_specs=placed,
        out_specs=(P(None, "sector", "box", None), P(None, "sector", "box", None)),
        check_vma=False,
    )
```

profile of v0, /device:TPU:2, one launch (start us, length us, event | category | flops | bytes accessed | tf_op | source)
XLA Modules:
  0.0 371.9 jit_solution(226998493648815140)
XLA Ops:
  9.0 3.4 copy.326
  12.5 2.7 copy.325
  15.2 3.0 gather_fusion.1
  20.1 2.9 gather_fusion
  26.3 3.6 collective-permute-start
  36.4 6.2 %constant_dynamic-slice_fusion.1 = (bf16[1,441,441]{2,0,1:T(2,128)(2,1)}, bf16[1,441,441]{2,0,1:T(2,128)(2,1)}, bf16[1,441,441]{2,0,1:T(2,128)(2,1)}, bf16[1,441...) fusion(bf16[2,441,441]{2,0,1:T(2,128)(2,1)S(1)} %copy-done.2, ...), kind=kLoop, calls=%fused_computation.812 | loop fusion | bytes 4667560 | tf_op jit(solution)/shard_map/jit(dynamic_index_in_dim)/dynamic_slice | solution.py:168
  42.6 4.9 %constant_dynamic-slice_fusion = (bf16[1,441,441]{2,0,1:T(2,128)(2,1)}, bf16[1,441,441]{2,0,1:T(2,128)(2,1)}, bf16[1,441,441]{2,0,1:T(2,128)(2,1)}, bf16[1,441,441]{2,0,1:T(2,128)(2,1)}) fusion(bf16[2,441,441]{2,0,1:T(2,128)(2,1)S(1)} %copy-done.3, s32[]{:T(128)S(6)} %select_n.162, s32[]{:T(128)S(6)} %select_n.161, s32[]{:T(128)S(6)} %select_n.160, ...), kind=kLoop, calls=%fused_computation.811 | loop fusion | bytes 3111712 | tf_op jit(solution)/shard_map/jit(dynamic_index_in_dim)/dynamic_slice | solution.py:169
  50.4 5.4 %fusion.134 = f32[64,3,21,21]{3,2,1,0:T(8,128)S(1)} fusion(f32[21,64,128]{2,0,1:T(8,128)} %copy.323, f32[3,64,128]{2,0,1:T(4,128)} %copy.322, f32[21,64,128,1]{2,1,0,3:T(8,128)} %bitcast.1389), kind=kOutput, calls=%fused_computation.243 | convolution fusion | flops 130572288 | bytes 1813248 | tf_op jit(solution)/shard_map/cjnp,knp->ncjk/dot_general | solution.py:58
  57.9 7.0 %gather_fusion.3 = bf16[16,441,441]{2,1,0:T(8,128)(2,1)} fusion(bf16[15,441,441]{2,1,0:T(8,128)(2,1)} %param.23, s32[1024]{0:T(1024)} %pad_clamp_fusion), kind=kCustom, calls=%fused_computation.3 | custom fusion | bytes 12446848 | tf_op jit(solution)/shard_map/gather | solution.py:163
  67.6 2.9 dot_general.193
  70.5 3.3 add_convert_fusion.1
  75.5 2.8 convert_element_type.236
  87.3 4.4 %collective-permute-start.7 = (bf16[3,441]{1,0:T(4,128)(2,1)S(1)}, bf16[3,441]{1,0:T(4,128)(2,1)S(1)}, u32[]{:S(2)}, u32[]{:S(2)}) collective-permute-start(bf16[3,441]{1,0:T(4,128)(2,1)S(1)} %fusion.240), channel_id=1, source_target_pairs={{0,4},{4,0},{1,5},{5,1},{2,6},{6,2},{3,7},{7,3},{8,12},{12,8},{9,1... | collective-permute-start | bytes 7946 | tf_op jit(solution)/shard_map/ppermute | solution.py:40
  91.7 25.5 %fusion.45 = (f32[64,128]{1,0:T(8,128)}, f32[64,128]{1,0:T(8,128)}, f32[64,128]{1,0:T(8,128)}, f32[64,128]{1,0:T(8,128)}, f32[64,128]{1,0:T(8,128)}, /*index=5*/f32[64,128]{1,0:T(8,128)}) fusion(f32[64,128]{1,0:T(8,128)S(1)} %get-tuple-element.166, f32[64,128]{1,0:T(8,128)S(1)} %get-tuple-element.167, f32[64,128]{1,0:T(8,128)S(1)} %get-tuple-element.168, ...), kind=kLoop, calls=%fused_computation.150 | loop fusion | flops 54476800 | bytes 688128 | tf_op jit(solution)/shard_map/while/body/eval_jaxpr/reduce_sum | solution.py:76
  119.0 3.4 collective-permute-start.8
  129.8 25.9 %all-gather.2 = bf16[16,3,441]{2,1,0:T(4,128)(2,1)S(1)} all-gather(bf16[1,3,441]{2,1,0:T(4,128)(2,1)S(1)} %fusion.266), channel_id=2, replica_groups=mesh['sector'=16,'box'=16] {'sector'}, dimensions={0}, use_global_device_ids=true | all-gather | bytes 44982 | tf_op jit(solution)/shard_map/all_gather | solution.py:160
  155.7 4.6 %fusion.262 = f32[3,441]{1,0:T(4,128)S(1)} fusion(bf16[16,441,441]{2,1,0:T(8,128)(2,1)} %gather_fusion.3, bf16[1,441,441]{2,0,1:T(2,128)(2,1)} %get-tuple-element.125, bf16[16,3,441]{2,1,0:T(4,128)(2,1)S(1)} %all-gather.2, pred[16]{0:T(512)(128)(4,1)} %fusion.434), kind=kOutput, calls=%fused_computation.344 | convolution fusion | flops 19859554 | bytes 6659998 | tf_op jit(solution)/shard_map/cy,xy->cx/dot_general | solution.py:170
  171.8 2.6 fusion.173
  175.6 3.3 reshape.4930
  178.9 6.0 %fusion.131 = f32[3,64,128]{2,0,1:T(4,128)S(1)} fusion(f32[64,3,21,21]{3,2,1,0:T(8,128)} %reshape.4930, f32[21,64,128]{2,0,1:T(8,128)} %copy.323, f32[21,64,128,1]{2,1,0,3:T(8,128)S(1)} %bitcast.1390), kind=kOutput, calls=%fused_computation.240 | convolution fusion | flops 131063808 | bytes 1813248 | tf_op jit(solution)/shard_map/ncjk,knp->cjnp/dot_general | solution.py:63
  186.2 28.9 %fusion.69 = (f32[64,128]{1,0:T(8,128)S(1)}, f32[64,128]{1,0:T(8,128)S(1)}, f32[64,128]{1,0:T(8,128)S(1)}, f32[64,128]{1,0:T(8,128)S(1)}, f32[64,128]{1,0:T(8,12...) fusion(f32[64,128]{1,0:T(8,128)S(1)} %get-tuple-element.142, ...), kind=kLoop, calls=%fused_computation.174 | loop fusion | flops 81715200 | bytes 884736 | tf_op jit(solution)/shard_map/while/body/eval_jaxpr/reduce_sum | solution.py:76
  219.3 5.5 %fusion.132 = f32[64,3,21,21]{3,2,1,0:T(8,128)} fusion(f32[21,64,128]{2,0,1:T(8,128)S(1)} %copy.364, f32[3,64,128]{2,0,1:T(4,128)S(1)} %copy-done.14, f32[21,64,128,1]{2,1,0,3:T(8,128)S(1)} %bitcast.1387), kind=kOutput, calls=%fused_computation.241 | convolution fusion | flops 130572288 | bytes 1813248 | tf_op jit(solution)/shard_map/cjnp,knp->ncjk/dot_general | solution.py:58
  224.9 3.3 copy.366
  244.4 2.6 copy.381
  248.4 3.0 collective-permute-start.9
  260.6 4.5 %collective-permute-start.16 = (bf16[3,441]{1,0:T(4,128)(2,1)S(1)}, bf16[3,441]{1,0:T(4,128)(2,1)S(1)}, u32[]{:S(2)}, u32[]{:S(2)}) collective-permute-start(bf16[3,441]{1,0:T(4,128)(2,1)S(1)} %fusion.249), channel_id=1, source_target_pairs={{0,8},{8,0},{1,9},{9,1},{2,10},{10,2},{3,11},{11,3},{4,12},{12,4},... | collective-permute-start | bytes 7946 | tf_op jit(solution)/shard_map/ppermute | solution.py:40
  265.1 24.4 %fusion.105 = (f32[64,128]{1,0:T(8,128)S(1)}, f32[64,128]{1,0:T(8,128)S(1)}, f32[64,128]{1,0:T(8,128)S(1)}, f32[64,128]{1,0:T(8,128)S(1)}, f32[64,128]{1,0:T(8,128)S(1)}, /*index=5*/f32[64,128]{1,0:T(8,128)}) fusion(f32[64,128]{1,0:T(8,128)S(1)} %get-tuple-element.154, f32[64,128]{1,0:T(8,128)S(1)} %get-tuple-element.155, ...), kind=kLoop, calls=%fused_computation.210 | loop fusion | flops 54476800 | bytes 688128 | tf_op jit(solution)/shard_map/while/body/eval_jaxpr/reduce_sum | solution.py:76
  289.8 25.9 %all-gather.3 = bf16[16,3,441]{2,1,0:T(4,128)(2,1)S(1)} all-gather(bf16[1,3,441]{2,1,0:T(4,128)(2,1)S(1)} %fusion.264), channel_id=3, replica_groups=mesh['sector'=16,'box'=16] {'sector'}, dimensions={0}, use_global_device_ids=true | all-gather | bytes 44982 | tf_op jit(solution)/shard_map/all_gather | solution.py:160
  315.7 4.6 %fusion.261 = f32[3,441]{1,0:T(4,128)S(1)} fusion(bf16[16,441,441]{2,1,0:T(8,128)(2,1)} %gather_fusion.3, bf16[1,441,441]{2,0,1:T(2,128)(2,1)} %get-tuple-element.125, bf16[16,3,441]{2,1,0:T(4,128)(2,1)S(1)} %all-gather.3, pred[16]{0:T(512)(128)(4,1)S(1)} %copy-done.61), kind=kOutput, calls=%fused_computation.343 | convolution fusion | flops 19859554 | bytes 6659998 | tf_op jit(solution)/shard_map/cy,xy->cx/dot_general | solution.py:170
  329.1 2.7 fusion.170
  335.5 5.2 %fusion.130 = f32[3,64,128]{2,0,1:T(4,128)S(1)} fusion(f32[64,3,21,21]{3,2,1,0:T(8,128)S(1)} %reshape.4932, f32[21,64,128]{2,0,1:T(8,128)S(1)} %copy-done.5, f32[21,64,128,1]{2,1,0,3:T(8,128)} %bitcast.1388), kind=kOutput, calls=%fused_computation.238 | convolution fusion | flops 131063808 | bytes 1813248 | tf_op jit(solution)/shard_map/ncjk,knp->cjnp/dot_general | solution.py:63
  341.8 28.9 %fusion.129 = (f32[64,128]{1,0:T(8,128)S(1)}, f32[64,128]{1,0:T(8,128)S(1)}, f32[64,128]{1,0:T(8,128)S(1)}, f32[64,128]{1,0:T(8,128)S(1)}, f32[64,128]{1,0:T(8,1...) fusion(f32[64,128]{1,0:T(8,128)S(1)} %get-tuple-element.130, ...), kind=kLoop, calls=%fused_computation.234 | loop fusion | flops 81715200 | bytes 884736 | tf_op jit(solution)/shard_map/while/body/eval_jaxpr/reduce_sum | solution.py:76
  (377 shorter events, 106.0 us)
Async XLA Ops:
  6.7 178.2 %collective-permute-start.3 = (bf16[6,1,64,128]{3,2,1,0:T(8,128)(2,1)}, bf16[6,1,64,128]{3,2,1,0:T(8,128)(2,1)}, u32[]{:S(2)}, u32[]{:S(2)}) collective-permute-start(bf16[6,1,64,128]{3,2,1,0:T(8,128)(2,1)} %get-tuple-element.196), channel_id=1, source_target_pairs={{16,0},{32,16},{48,32},{64,48},{80,64},{96,80},{112,96},{128,112},... | collective-permute-start | bytes 294920 | tf_op jit(solution)/shard_map/ppermute | solution.py:28
  9.0 176.0 %collective-permute-start.2 = (bf16[6,1,64,128]{3,2,1,0:T(8,128)(2,1)}, bf16[6,1,64,128]{3,2,1,0:T(8,128)(2,1)}, u32[]{:S(2)}, u32[]{:S(2)}) collective-permute-start(bf16[6,1,64,128]{3,2,1,0:T(8,128)(2,1)} %get-tuple-element.196), channel_id=1, source_target_pairs={{0,16},{16,32},{32,48},{48,64},{64,80},{80,96},{96,112},{112,128},... | collective-permute-start | bytes 294920 | tf_op jit(solution)/shard_map/ppermute | solution.py:27
  15.2 21.2 %copy-start.2 = (bf16[2,441,441]{2,0,1:T(2,128)(2,1)S(1)}, bf16[2,441,441]{2,0,1:T(2,128)(2,1)}, u32[]{:S(2)}) copy-start(bf16[2,441,441]{2,0,1:T(2,128)(2,1)} %param.21) | copy-start | bytes 2333776
  23.1 41.9 %collective-permute-start.4 = (f32[6,256]{1,0:T(8,128)S(1)}, f32[6,256]{1,0:T(8,128)S(1)}, u32[]{:S(2)}, u32[]{:S(2)}) collective-permute-start(f32[6,256]{1,0:T(8,128)S(1)} %pad_maximum_fusion.6), channel_id=1, source_target_pairs={{0,16},{16,32},{32,48},{48,64},{64,80},{80,96},{96,112},{112,128},... | collective-permute-start | bytes 18440 | tf_op jit(solution)/shard_map/ppermute | solution.py:45
  25.0 57.1 %collective-permute-start.1 = (bf16[6,1,1,128]{3,2,0,1:T(2,128)(2,1)}, bf16[6,1,1,128]{3,2,0,1:T(2,128)(2,1)}, u32[]{:S(2)}, u32[]{:S(2)}) collective-permute-start(bf16[6,1,1,128]{3,2,0,1:T(2,128)(2,1)} %get-tuple-element.192), channel_id=1, source_target_pairs={{1,0},{2,1},{3,2},{4,3},{5,4},{6,5},{7,6},{8,7},{9,8},{10,9},{11,1... | collective-permute-start | bytes 4616 | tf_op jit(solution)/shard_map/ppermute | solution.py:28
  26.3 55.9 %collective-permute-start = (bf16[6,1,1,128]{3,2,0,1:T(2,128)(2,1)}, bf16[6,1,1,128]{3,2,0,1:T(2,128)(2,1)}, u32[]{:S(2)}, u32[]{:S(2)}) collective-permute-start(bf16[6,1,1,128]{3,2,0,1:T(2,128)(2,1)} %get-tuple-element.191), channel_id=1, source_target_pairs={{0,1},{1,2},{2,3},{3,4},{4,5},{5,6},{6,7},{7,8},{8,9},{9,10},{10,1... | collective-permute-start | bytes 4616 | tf_op jit(solution)/shard_map/ppermute | solution.py:27
  81.2 1.8 collective-permute-start.5
  83.3 3.6 collective-permute-start.6
  87.3 30.8 %collective-permute-start.7 = (bf16[3,441]{1,0:T(4,128)(2,1)S(1)}, bf16[3,441]{1,0:T(4,128)(2,1)S(1)}, u32[]{:S(2)}, u32[]{:S(2)}) collective-permute-start(bf16[3,441]{1,0:T(4,128)(2,1)S(1)} %fusion.240), channel_id=1, source_target_pairs={{0,4},{4,0},{1,5},{5,1},{2,6},{6,2},{3,7},{7,3},{8,12},{12,8},{9,1... | collective-permute-start | bytes 7946 | tf_op jit(solution)/shard_map/ppermute | solution.py:40
  119.0 9.1 %collective-permute-start.8 = (bf16[3,441]{1,0:T(4,128)(2,1)}, bf16[3,441]{1,0:T(4,128)(2,1)}, u32[]{:S(2)}, u32[]{:S(2)}) collective-permute-start(bf16[3,441]{1,0:T(4,128)(2,1)} %fusion.241), channel_id=1, source_target_pairs={{0,8},{8,0},{1,9},{9,1},{2,10},{10,2},{3,11},{11,3},{4,12},{12,4},... | collective-permute-start | bytes 7946 | tf_op jit(solution)/shard_map/ppermute | solution.py:40
  184.9 31.1 %copy-start.15 = (f32[3,64,128]{2,0,1:T(4,128)}, f32[3,64,128]{2,0,1:T(4,128)S(1)}, u32[]{:S(2)}) copy-start(f32[3,64,128]{2,0,1:T(4,128)S(1)} %fusion.131) | copy-start | bytes 294916
  184.9 30.4 %copy-start.26 = (f32[64,128]{1,0:T(8,128)S(1)}, f32[64,128]{1,0:T(8,128)}, u32[]{:S(2)}) copy-start(f32[64,128]{1,0:T(8,128)} %get-tuple-element.80) | copy-start | bytes 98308
  184.9 30.4 %copy-start.27 = (f32[64,128]{1,0:T(8,128)S(1)}, f32[64,128]{1,0:T(8,128)}, u32[]{:S(2)}) copy-start(f32[64,128]{1,0:T(8,128)} %get-tuple-element.81) | copy-start | bytes 98308
  184.9 30.4 %copy-start.28 = (f32[64,128]{1,0:T(8,128)S(1)}, f32[64,128]{1,0:T(8,128)}, u32[]{:S(2)}) copy-start(f32[64,128]{1,0:T(8,128)} %get-tuple-element.82) | copy-start | bytes 98308
  184.9 30.4 %copy-start.29 = (f32[64,128]{1,0:T(8,128)S(1)}, f32[64,128]{1,0:T(8,128)}, u32[]{:S(2)}) copy-start(f32[64,128]{1,0:T(8,128)} %get-tuple-element.107) | copy-start | bytes 98308
  184.9 30.4 %copy-start.30 = (f32[64,128]{1,0:T(8,128)S(1)}, f32[64,128]{1,0:T(8,128)}, u32[]{:S(2)}) copy-start(f32[64,128]{1,0:T(8,128)} %get-tuple-element.108) | copy-start | bytes 98308
  184.9 30.4 %copy-start.31 = (f32[64,128]{1,0:T(8,128)S(1)}, f32[64,128]{1,0:T(8,128)}, u32[]{:S(2)}) copy-start(f32[64,128]{1,0:T(8,128)} %get-tuple-element.109) | copy-start | bytes 98308
  184.9 31.1 %copy-start.6 = (f32[21,64,128]{2,1,0:T(8,128)S(1)}, f32[21,64,128]{2,1,0:T(8,128)}, u32[]{:S(2)}) copy-start(f32[21,64,128]{2,1,0:T(8,128)} %get-tuple-element.217) | copy-start | bytes 2064388
  185.0 31.1 %copy-start.20 = (f32[21,64,128]{2,1,0:T(8,128)S(1)}, f32[21,64,128]{2,1,0:T(8,128)}, u32[]{:S(2)}) copy-start(f32[21,64,128]{2,1,0:T(8,128)} %get-tuple-element.218) | copy-start | bytes 2064388
  186.2 33.1 %copy-start.14 = (f32[3,64,128]{2,0,1:T(4,128)S(1)}, f32[3,64,128]{2,0,1:T(4,128)}, u32[]{:S(2)}) copy-start(f32[3,64,128]{2,0,1:T(4,128)} %copy.322) | copy-start | bytes 294916
  234.4 106.3 %collective-permute-start.12 = (bf16[6,1,64,128]{3,2,1,0:T(8,128)(2,1)}, bf16[6,1,64,128]{3,2,1,0:T(8,128)(2,1)}, u32[]{:S(2)}, u32[]{:S(2)}) collective-permute-start(bf16[6,1,64,128]{3,2,1,0:T(8,128)(2,1)} %pad_maximum_fusion.2), channel_id=1, source_target_pairs={{16,0},{32,16},{48,32},{64,48},{80,64},{96,80},{112,96},{128,112},... | collective-permute-start | bytes 294920 | tf_op jit(solution)/shard_map/ppermute | solution.py:28
  236.4 104.3 %collective-permute-start.11 = (bf16[6,1,64,128]{3,2,1,0:T(8,128)(2,1)}, bf16[6,1,64,128]{3,2,1,0:T(8,128)(2,1)}, u32[]{:S(2)}, u32[]{:S(2)}) collective-permute-start(bf16[6,1,64,128]{3,2,1,0:T(8,128)(2,1)} %pad_maximum_fusion.2), channel_id=1, source_target_pairs={{0,16},{16,32},{32,48},{48,64},{64,80},{80,96},{96,112},{112,128},... | collective-permute-start | bytes 294920 | tf_op jit(solution)/shard_map/ppermute | solution.py:27
  241.1 10.3 %collective-permute-start.13 = (bf16[3,441]{1,0:T(4,128)(2,1)S(1)}, bf16[3,441]{1,0:T(4,128)(2,1)S(1)}, u32[]{:S(2)}, u32[]{:S(2)}) collective-permute-start(bf16[3,441]{1,0:T(4,128)(2,1)S(1)} %fusion.236), channel_id=1, source_target_pairs={{0,1},{1,0},{2,3},{3,2},{4,5},{5,4},{6,7},{7,6},{8,9},{9,8},{10,11... | collective-permute-start | bytes 7946 | tf_op jit(solution)/shard_map/ppermute | solution.py:40
  244.4 20.7 %copy-start.55 = (f32[64,128]{1,0:T(8,128)S(1)}, f32[64,128]{1,0:T(8,128)}, u32[]{:S(2)}) copy-start(f32[64,128]{1,0:T(8,128)} %get-tuple-element.184) | copy-start | bytes 98308
  247.1 6.4 %collective-permute-start.10 = (bf16[6,1,1,128]{3,2,1,0:T(2,128)(2,1)}, bf16[6,1,1,128]{3,2,1,0:T(2,128)(2,1)S(1)}, u32[]{:S(2)}, u32[]{:S(2)}) collective-permute-start(bf16[6,1,1,128]{3,2,1,0:T(2,128)(2,1)} %get-tuple-element.179), channel_id=1, source_target_pairs={{1,0},{2,1},{3,2},{4,3},{5,4},{6,5},{7,6},{8,7},{9,8},{10,9},{11,1... | collective-permute-start | bytes 4616 | tf_op jit(solution)/shard_map/ppermute | solution.py:28
  248.4 5.0 %collective-permute-start.9 = (bf16[6,1,1,128]{3,2,1,0:T(2,128)(2,1)S(1)}, bf16[6,1,1,128]{3,2,1,0:T(2,128)(2,1)S(1)}, u32[]{:S(2)}, u32[]{:S(2)}) collective-permute-start(bf16[6,1,1,128]{3,2,1,0:T(2,128)(2,1)S(1)} %get-tuple-element.178), channel_id=1, source_target_pairs={{0,1},{1,2},{2,3},{3,4},{4,5},{5,6},{6,7},{7,8},{8,9},{9,10},{10,1... | collective-permute-start | bytes 4616 | tf_op jit(solution)/shard_map/ppermute | solution.py:27
  251.6 64.1 %copy-start.61 = (pred[16]{0:T(512)(128)(4,1)S(1)}, pred[16]{0:T(512)(128)(4,1)}, u32[]{:S(2)}) copy-start(pred[16]{0:T(512)(128)(4,1)} %fusion.434) | copy-start | bytes 52
  251.8 3.6 collective-permute-start.14
  255.7 4.5 %collective-permute-start.15 = (bf16[3,441]{1,0:T(4,128)(2,1)S(1)}, bf16[3,441]{1,0:T(4,128)(2,1)S(1)}, u32[]{:S(2)}, u32[]{:S(2)}) collective-permute-start(bf16[3,441]{1,0:T(4,128)(2,1)S(1)} %fusion.248), channel_id=1, source_target_pairs={{0,4},{4,0},{1,5},{5,1},{2,6},{6,2},{3,7},{7,3},{8,12},{12,8},{9,1... | collective-permute-start | bytes 7946 | tf_op jit(solution)/shard_map/ppermute | solution.py:40
  260.6 28.9 %collective-permute-start.16 = (bf16[3,441]{1,0:T(4,128)(2,1)S(1)}, bf16[3,441]{1,0:T(4,128)(2,1)S(1)}, u32[]{:S(2)}, u32[]{:S(2)}) collective-permute-start(bf16[3,441]{1,0:T(4,128)(2,1)S(1)} %fusion.249), channel_id=1, source_target_pairs={{0,8},{8,0},{1,9},{9,1},{2,10},{10,2},{3,11},{11,3},{4,12},{12,4},... | collective-permute-start | bytes 7946 | tf_op jit(solution)/shard_map/ppermute | solution.py:40
  340.7 30.0 %copy-start.24 = (f32[3,1,64,128]{3,2,1,0:T(8,128)S(1)}, f32[3,1,64,128]{3,2,1,0:T(8,128)}, u32[]{:S(2)}) copy-start(f32[3,1,64,128]{3,2,1,0:T(8,128)} %get-tuple-element.115) | copy-start | bytes 294916
  340.7 30.0 %copy-start.41 = (f32[64,128]{1,0:T(8,128)S(1)}, f32[64,128]{1,0:T(8,128)}, u32[]{:S(2)}) copy-start(f32[64,128]{1,0:T(8,128)} %get-tuple-element.100) | copy-start | bytes 98308
  (48 other events, 405.5 us)
where the time goes:
time: 379 us; the launch traced here: 372 us
  other arithmetic  128 us (34%)
  local copies, waits for them, and re-layouts  79.9 us (21%)
  matrix products  69.6 us (18%)
  blocking collectives  51.8 us (14%)
  starting transfers between devices  34.2 us (9%)
  waiting for transfers between devices  5.86 us (2%)
    reduce_sum x4, other arithmetic, pair_velocity(): jnp.sum(inverse * (weight_y * delta_z - weight_z * delta_y), axis=2)  108 us
    all_gather x2, blocking collectives, far_field(): piece = lax.all_gather(current[None], 'sector', axis=0, tiled=True)  51.8 us
    dot_general x8, matrix products, far_field(): jnp.einsum('cy,xy->cx', local, up_side, preferred_element_type=jnp.float32)  19.6 us
    ppermute x8, starting transfers between devices, partner_2(): return lax.ppermute(block, axis, route)  19.4 us
    dot_general x2, matrix products, evaluate(): jnp.einsum('ncjk,knp->cjnp', shaped, cheb_b, precision=HIGHEST_PRECISION)  11.1 us
    dot_general x2, matrix products, multipoles(): jnp.einsum('cjnp,knp->ncjk', weighted, cheb_b, precision=HIGHEST_PRECISION)  10.9 us
    convert_element_type x6, local copies, waits for them, and re-layouts, far_field(): leaf = (multipoles(cheb_a, cheb_b, weights) + arrival_terms).reshape(box_...  10 us
    reshape x4, local copies, waits for them, and re-layouts, far_field(): presum = presum.astype(jnp.bfloat16).reshape(NCLASS, box_count * 3, coef)  8.64 us
  transfers between devices with their start and end apart: 17, of which 4 were waited for; matrix products, arithmetic and copies ran while one was open for 52% of the time, Pallas kernels for 0%

commit v1 on v0

v1 whole, which is shorter than its diff:
```python
import functools
import math

import jax
import jax.numpy as jnp
from jax import lax
from jax.experimental import pallas as pl
from jax.experimental.pallas import tpu as pltpu
from jax.sharding import PartitionSpec as P

TERMS = 21
COEF = TERMS * TERMS
PAD = 24
ROWS = 512
BOXES = 64
SLOTS = 128
CROSS = 256
NCLASS = 4
GROUP = 16
DELTA_SQ = 0.25
TIME_STEP = 0.02
INV_FOUR_PI = 1.0 / (4.0 * math.pi)
OFFSETS = ((0.0, 0.0, 0.0), (0.0, 0.0, -2.0), (0.0, 0.0, 2.0), (-2.0, 0.0, 0.0), (2.0, 0.0, 0.0))
BF16 = jnp.bfloat16
F32 = jnp.float32
MESH = pl.DeviceIdType.MESH

NN = (((1,), (0,)), ((), ()))
NT = (((1,), (1,)), ((), ()))


def mm(a, b):
    return lax.dot_general(a, b, NN, preferred_element_type=F32)


def mm_t(a, b):
    return lax.dot_general(a, b, NT, preferred_element_type=F32)


def rounded(value):
    return value.astype(BF16).astype(F32)


def iota(shape, dim):
    return lax.broadcasted_iota(jnp.int32, shape, dim)


def one_where(condition, dtype=F32):
    return jnp.where(condition, 1.0, 0.0).astype(dtype)


def reversed_digits(index):
    return (index & 3) * 16 + ((index >> 2) & 3) * 4 + (index >> 4)


def kernel(
    pos_ref, str_ref, cnt_ref, cross_ref, arr_ref, ils_ref, ilc_ref,
    m2m_hbm, m2l_hbm, up_hbm, tm_hbm, sec_hbm,
    outp_ref, outv_ref,
    m2m, m2l, up, tm, sec,
    weights, places, halo_p, halo_w, end_out, end_in, leave_out, leave_in,
    src_f, src_s, tgt_f, cheb_a, cheb_b, arr_a, arr_b, phi_ref,
    leaf_box, local_box, near_box, far_box,
    arr_leaf, leaf504, leaf441, select, counts_pc, presum, translated,
    up1, up2, root, pack_f, root_out, root_in, tree_e, tree_o, down1, down2, down3,
    sec_out, sec_in,
    load_sem, send_sem, recv_sem,
):
    s_id = lax.axis_index("sector")
    g_id = lax.axis_index("box")

    loads = []
    for index, (src, dst) in enumerate(((m2m_hbm, m2m), (up_hbm, up), (m2l_hbm, m2l), (tm_hbm, tm), (sec_hbm, sec))):
        copy = pltpu.make_async_copy(src, dst, load_sem.at[index])
        copy.start()
        loads.append(copy)

    def box_peer(distance):
        total = 0
        for bit in range(4):
            mine = (g_id // (1 << bit)) % 2
            total = total + ((mine + (distance >> bit & 1)) % 2) * (1 << bit)
        return (s_id, total)

    def sector_peer(distance):
        return ((s_id + distance) % GROUP, g_id)

    barrier = pltpu.get_barrier_semaphore()
    for distance in range(1, GROUP):
        pl.semaphore_signal(barrier, inc=1, device_id=box_peer(distance), device_id_type=MESH)
        pl.semaphore_signal(barrier, inc=1, device_id=sector_peer(distance), device_id_type=MESH)
    before = (s_id, (g_id + GROUP - 1) % GROUP)
    after = (s_id, (g_id + 1) % GROUP)

    next_sem = [0]
    sends = []

    def remote(src, dst, device):
        index = next_sem[0]
        next_sem[0] += 1
        copy = pltpu.make_async_remote_copy(
            src_ref=src, dst_ref=dst, send_sem=send_sem.at[index], recv_sem=recv_sem.at[index],
            device_id=device, device_id_type=MESH,
        )
        copy.start()
        sends.append(copy)
        return copy

    diagonal = iota((BOXES, BOXES), 0) == iota((BOXES, BOXES), 1)
    count_col = jnp.sum(jnp.where(diagonal, jnp.broadcast_to(cnt_ref[...].astype(F32), (BOXES, BOXES)), 0.0), axis=1, keepdims=True)
    present = one_where(iota((BOXES, SLOTS), 1).astype(F32) < count_col)
    crossing = cross_ref[...]
    hit_box = one_where(iota((BOXES, CROSS), 0) == (crossing >> 7), BF16)
    hit_slot = one_where(iota((SLOTS, CROSS), 0) == (crossing & 127))
    departed = mm_t(hit_box, hit_slot.astype(BF16))
    live = present * (1.0 - departed)
    leave_out[...] = jnp.zeros_like(leave_out)
    for c in range(3):
        weights[c] = str_ref[c] * live
    for c in range(6):
        value = pos_ref[c] if c < 3 else str_ref[c - 3] * present
        turned = value.T
        high = turned.astype(BF16)
        rest = turned - high.astype(F32)
        middle = rest.astype(BF16)
        low = (rest - middle.astype(F32)).astype(BF16)
        picked = mm(high, hit_box) + mm(middle, hit_box) + mm(low, hit_box)
        leave_out[c : c + 1, :] = jnp.sum(picked * hit_slot, axis=0, keepdims=True)

    def fill_ends(step, place):
        end_out[step] = jnp.zeros((2, 8, SLOTS), F32)
        for c in range(3):
            end_out[step, 0, c : c + 1, :] = place[c, BOXES - 1 : BOXES, :]
            end_out[step, 1, c : c + 1, :] = place[c, 0:1, :]
            end_out[step, 0, 3 + c : 4 + c, :] = weights[c, BOXES - 1 : BOXES, :]
            end_out[step, 1, 3 + c : 4 + c, :] = weights[c, 0:1, :]

    fill_ends(0, pos_ref)
    pl.semaphore_wait(barrier, 2 * (GROUP - 1))
    got_leave = remote(leave_out, leave_in, sector_peer(1))

    def send_halo(step, place):
        return [
            remote(place, halo_p.at[step, 0], sector_peer(1)),
            remote(place, halo_p.at[step, 1], sector_peer(GROUP - 1)),
            remote(end_out.at[step, 0], end_in.at[step, 0], after),
            remote(end_out.at[step, 1], end_in.at[step, 1], before),
        ]

    got_weights = [
        remote(weights, halo_w.at[0], sector_peer(1)),
        remote(weights, halo_w.at[1], sector_peer(GROUP - 1)),
    ]
    got_halo = send_halo(0, pos_ref)

    row = iota((ROWS, ROWS), 0)
    order = (row * 2731) >> 16
    select[...] = one_where((iota((ROWS, ROWS), 1) == row - 3 * order) & (row - PAD * order < TERMS) & (order < TERMS), BF16)
    for ref in (cheb_a, cheb_b, arr_a, arr_b, up1, up2, root, pack_f, tree_e, tree_o, down1, down2, local_box):
        ref[...] = jnp.zeros_like(ref)

    permute = one_where(reversed_digits(iota((BOXES, BOXES), 0)) == iota((BOXES, BOXES), 1), BF16)
    code = mm(permute, (ils_ref[...] + BOXES * ilc_ref[...]).astype(F32).astype(BF16))
    source = reversed_digits(iota((BOXES, BOXES), 1)).astype(F32)
    for kind in range(NCLASS):
        wanted = source + float(BOXES * kind)
        total = jnp.zeros((BOXES, BOXES), F32)
        for entry in range(16):
            total = total + one_where(code[:, entry : entry + 1] == wanted)
        counts_pc[kind * BOXES : (kind + 1) * BOXES, :] = total.astype(BF16)

    def split(value):
        high = rounded(value)
        return high, value - high

    def put_targets(x, y, z):
        rows = []
        halves = [split(v) for v in (x, y, z)]
        rows += [h for h, _ in halves] * 2 + [l for _, l in halves]
        norm = x * x + y * y + z * z
        n1, rest = split(norm)
        n2, n3 = split(rest)
        rows += [n1, n2, n3]
        for index, value in enumerate(rows):
            tgt_f[pl.ds(index, BOXES, stride=16), :] = value

    def put_sources(kind, base, count, coords, weight):
        offset = OFFSETS[kind]
        x, y, z = (v + o if o else v for v, o in zip(coords, offset))
        halves = [split(-2.0 * v) for v in (x, y, z)]
        highs = [h for h, _ in halves]
        m1, rest = split(x * x + y * y + z * z + DELTA_SQ)
        m2, m3 = split(rest)
        ones = jnp.ones_like(x)
        rows = highs + [l for _, l in halves] + highs + [ones] * 3 + [m1, m2, m3, jnp.zeros_like(x)]
        wx, wy, wz = weight
        moments = [wx, wy, wz, wy * z - wz * y, wz * x - wx * z, wx * y - wy * x]
        parts = [split(v) for v in moments]
        zero = jnp.zeros_like(x)
        sums = [h for h, _ in parts] + [zero] * 2 + [l for _, l in parts] + [zero] * 2
        for index in range(16):
            if count == 1:
                spot = slice(base * 16 + index, base * 16 + index + 1)
            else:
                spot = pl.ds(base * 16 + index, count, stride=16)
            src_f[kind, spot, :] = rows[index]
            src_s[kind, spot, :] = sums[index]

    for index in range(12, 16):
        tgt_f[pl.ds(index, BOXES, stride=16), :] = jnp.full((BOXES, SLOTS), 1.0 if index < 15 else 0.0, F32)

    def series(coordinate, put):
        scaled = 0.5 * coordinate
        older, newer = jnp.ones_like(scaled), scaled
        put(0, older)
        put(1, newer)
        for index in range(2, TERMS):
            older, newer = newer, 2.0 * scaled * newer - older
            put(index, newer)

    def own_terms(place):
        x, y, z = place[0], place[1], place[2]
        weight = (weights[0], weights[1], weights[2])
        put_targets(x, y, z)
        put_sources(0, 0, BOXES, (x, y, z), weight)
        put_sources(1, 1, BOXES, (x, y, z), weight)
        put_sources(2, 0, BOXES, (x, y, z), weight)

        def put_a(index, value):
            cheb_a[pl.ds(index, BOXES, stride=PAD), :] = value

        def put_b(index, value):
            cheb_b[pl.ds(index, BOXES, stride=PAD), :] = value

        series(x, put_a)
        series(y, put_b)

    def halo_terms(step):
        for side in range(2):
            got_halo[side].wait_recv()
            if step == 0:
                got_weights[side].wait_recv()
            coords = tuple(halo_p[step, side, c] for c in range(3))
            weight = tuple(halo_w[side, c] for c in range(3))
            put_sources(3 + side, 0, BOXES, coords, weight)
        for side in range(2):
            got_halo[2 + side].wait_recv()
            inside = (g_id > 0) if side == 0 else (g_id < GROUP - 1)
            keep = jnp.where(inside, 1.0, 0.0).astype(F32)
            coords = tuple(end_in[step, side, c : c + 1, :] for c in range(3))
            weight = tuple(end_in[step, side, 3 + c : 4 + c, :] * keep for c in range(3))
            put_sources(1 + side, 0 if side == 0 else BOXES, 1, coords, weight)

    def basis(a_row, b_block, width):
        pieces = []
        for index in range(0, TERMS - 1, 2):
            pair = jnp.concatenate([a_row(index) * b_block, a_row(index + 1) * b_block], axis=0)
            pieces.append(pair.astype(BF16))
        last = jnp.concatenate([a_row(TERMS - 1) * b_block, jnp.zeros((8, width), F32)], axis=0)
        pieces.append(last.astype(BF16))
        return jnp.concatenate(pieces, axis=0)

    def box_order(box):
        return (box % 4) * 16 + ((box // 4) % 4) * 4 + box // 16

    def leaf_step(box, carry):
        start = pl.multiple_of(box * PAD, 8)
        b_block = cheb_b[pl.ds(start, PAD), :]
        phi = basis(lambda j: cheb_a[pl.ds(start + j, 1), :], b_block, SLOTS)
        phi_ref[box] = phi
        lhs = src_s[0, pl.ds(pl.multiple_of(box * 16, 16), 16), :].astype(BF16)
        got = mm_t(lhs, phi)
        got = got[0:8] + got[8:16]
        spot = pl.ds(pl.multiple_of(box_order(box) * 8, 8), 8)
        for t in range(4):
            leaf_box[t, spot, :] = got[:, t * 128 : (t + 1) * 128]
        return carry

    def arrival_terms():
        got_leave.wait_recv()

        def put_a(index, value):
            arr_a[index : index + 1, :] = value

        def put_b(index, value):
            arr_b[index : index + 1, :] = value

        series(leave_in[0:1, :], put_a)
        series(leave_in[1:2, :], put_b)
        phi = basis(lambda j: arr_a[j : j + 1, :], arr_b[...], CROSS)
        landing = one_where(reversed_digits(iota((BOXES, CROSS), 0)) == arr_ref[...])
        for c in range(3):
            high, low = split(landing * leave_in[3 + c : 4 + c, :])
            arr_leaf[c * BOXES : (c + 1) * BOXES, :] = mm_t(high.astype(BF16), phi) + mm_t(low.astype(BF16), phi)

    def make_leaf():
        for c in range(3):
            rows = slice(c * BOXES, (c + 1) * BOXES)
            for t in range(4):
                lanes = slice(t * 128, (t + 1) * 128)
                own = leaf_box[t, pl.ds(c, BOXES, stride=8), :]
                leaf504[rows, lanes] = (own + arr_leaf[rows, lanes]).astype(BF16)
        leaf441[...] = mm(leaf504[...], select[...]).astype(BF16)

    def pack(value, out):
        root[:, 0:COEF] = value
        for t in range(4):
            pack_f[t * 4 : t * 4 + 3, :] = root[0:3, t * 128 : (t + 1) * 128]
        out[...] = pack_f[...].astype(BF16)

    def upward():
        total = None
        for o in range(4):
            lhs = jnp.concatenate([leaf441[c * BOXES + o * 16 : c * BOXES + o * 16 + 16, 0:COEF] for c in range(3)], axis=0)
            part = mm(lhs, m2m[o])
            total = part if total is None else total + part
        level = rounded(total)
        for o in range(4):
            for c in range(3):
                up1[o, c * 4 : c * 4 + 4, 0:COEF] = level[c * 16 + o * 4 : c * 16 + o * 4 + 4]
        total = None
        for o in range(4):
            part = mm(up1[o, :, 0:COEF].astype(BF16), m2m[o])
            total = part if total is None else total + part
        level = rounded(total)
        for o in range(4):
            for c in range(3):
                up2[o, c : c + 1, 0:COEF] = level[c * 4 + o : c * 4 + o + 1]
        total = None
        for o in range(4):
            part = mm(up2[o, :, 0:COEF].astype(BF16), m2m[o])
            total = part if total is None else total + part
        return total

    def bit(level):
        return (g_id // (1 << level)) % 2

    def spread(index, ref, spot):
        value = ref[index].astype(F32)
        for t in range(4):
            spot[0][spot[1] * 4 : spot[1] * 4 + 4, t * 128 : (t + 1) * 128] = value[t * 4 : t * 4 + 4]

    def tree(step):
        for distance in range(GROUP):
            half = distance // 2
            spot = (half & 1) * 4 + (half >> 1 & 1) * 2 + (half >> 2)
            spread(distance, root_in.at[step], (tree_o if distance & 1 else tree_e, spot))
        lower = tree_e[:, 0:COEF].astype(BF16)
        upper = tree_o[:, 0:COEF].astype(BF16)
        siblings = []
        for level in range(4):
            siblings.append(upper[0:8] if upper.shape[0] >= 8 else upper)
            merged = mm(lower, up[bit(level)]) + mm(upper, up[1 - bit(level)])
            if level < 3:
                half = merged.shape[0] // 2
                lower = merged[0:half].astype(BF16)
                upper = merged[half:].astype(BF16)
        return merged, siblings

    def translate():
        for c in range(3):
            got = mm(counts_pc[...], leaf441[c * BOXES : (c + 1) * BOXES, :]).astype(BF16)
            for kind in range(NCLASS):
                presum[kind, c * BOXES : (c + 1) * BOXES, :] = got[kind * BOXES : (kind + 1) * BOXES]
        total = None
        for kind in range(NCLASS):
            part = mm(presum[kind, :, 0:COEF], m2l[kind])
            total = part if total is None else total + part
        translated[:, 0:COEF] = total

    def near_step(box, carry):
        own = pl.ds(pl.multiple_of(box * 16, 16), 16)
        later = pl.ds(pl.multiple_of(box * 16 + 16, 16), 16)
        target = tgt_f[own, :].T.astype(BF16)
        total = jnp.zeros((16, SLOTS), F32)
        for kind in range(5):
            spot = later if kind == 2 else own
            radius_sq = mm(target, src_f[kind, spot, :].astype(BF16))
            inverse = lax.rsqrt(radius_sq)
            cubed = (inverse * inverse * inverse).astype(BF16)
            total = total + mm_t(src_s[kind, spot, :].astype(BF16), cubed)
        near_box[pl.ds(pl.multiple_of(box * 8, 8), 8), :] = total[0:8] + total[8:16]
        return carry

    def downward(local):
        local = local.astype(BF16)
        for o in range(4):
            part = rounded(mm_t(local, m2m[o]))
            for c in range(3):
                down1[c * 4 + o : c * 4 + o + 1, 0:COEF] = part[c : c + 1]
        level = down1[:, 0:COEF].astype(BF16)
        for o in range(4):
            part = rounded(mm_t(level, m2m[o]))
            for c in range(3):
                down2[c * 16 + o * 4 : c * 16 + o * 4 + 4, 0:COEF] = part[c * 4 : c * 4 + 4]
        level = down2[:, 0:COEF].astype(BF16)
        for o in range(4):
            part = mm_t(level, m2m[o])
            for c in range(3):
                rows = slice(c * BOXES + o * 16, c * BOXES + o * 16 + 16)
                down3[rows, 0:COEF] = part[c * 16 : c * 16 + 16] + translated[rows, 0:COEF]
        high, low = split(down3[:, 0:COEF])
        chosen = select[:, 0:COEF]
        final = mm_t(high.astype(BF16), chosen) + mm_t(low.astype(BF16), chosen)
        for c in range(3):
            for t in range(4):
                local_box[t, pl.ds(c, BOXES, stride=8), :] = final[c * BOXES : (c + 1) * BOXES, t * 128 : (t + 1) * 128]

    def far_step(box, carry):
        spot = pl.ds(pl.multiple_of(box_order(box) * 8, 8), 8)
        value = jnp.concatenate([local_box[t, spot, :] for t in range(4)], axis=1)
        high, low = split(value)
        lhs = jnp.concatenate([high, low], axis=0).astype(BF16)
        got = mm(lhs, phi_ref[box])
        far_box[pl.ds(pl.multiple_of(box * 8, 8), 8), :] = got[0:8] + got[8:16]
        return carry

    for step in range(2):
        place = pos_ref if step == 0 else places
        if step == 1:
            fill_ends(1, places)
            got_halo = send_halo(1, places)
        own_terms(place)
        lax.fori_loop(0, BOXES, leaf_step, 0)
        if step == 0:
            arrival_terms()
            loads[0].wait()
        make_leaf()
        pack(upward(), root_out.at[step])
        root_in[step, 0] = root_out[step]
        got_roots = [
            remote(root_out.at[step], root_in.at[step, distance], box_peer(distance)) for distance in range(1, GROUP)
        ]
        if step == 0:
            for copy in loads[1:]:
                copy.wait()
        translate()
        halo_terms(step)
        lax.fori_loop(0, BOXES // 2, near_step, 0)
        for copy in got_roots:
            copy.wait_recv()
        top, siblings = tree(step)
        pack(jnp.concatenate([top, jnp.zeros((4, COEF), F32)], axis=0), sec_out.at[step])
        got_sectors = [
            remote(sec_out.at[step], sec_in.at[step, distance - 1], sector_peer(distance)) for distance in range(1, GROUP)
        ]
        crossed = [mm(siblings[level], tm[bit(level)])[0:4] for level in range(4)]
        lax.fori_loop(BOXES // 2, BOXES, near_step, 0)
        for copy in got_sectors:
            copy.wait_recv()
        total = jnp.zeros((4, COEF), F32)
        for distance in range(1, GROUP):
            spread(distance - 1, sec_in.at[step], (root, 0))
            total = total + mm(root[0:4, 0:COEF].astype(BF16), sec[GROUP - 1 - distance])
        local = total
        for level in reversed(range(4)):
            local = mm_t(local.astype(BF16), up[bit(level)]) + crossed[level]
        downward(local)
        lax.fori_loop(0, BOXES, far_step, 0)
        near = [near_box[pl.ds(c, BOXES, stride=8), :] for c in range(6)]
        x, y, z = place[0], place[1], place[2]
        swept = (
            near[1] * z - near[2] * y - near[3],
            near[2] * x - near[0] * z - near[4],
            near[0] * y - near[1] * x - near[5],
        )
        for c in range(3):
            velocity = INV_FOUR_PI * swept[c] + far_box[pl.ds(c, BOXES, stride=8), :] / float(TERMS)
            if step == 0:
                places[c] = place[c] + TIME_STEP * velocity
            else:
                outp_ref[c] = place[c] + TIME_STEP * velocity
                outv_ref[c] = velocity

    for copy in sends:
        copy.wait_send()


def per_device(positions, strengths, counts, cross_slot, arrive_box, il_source, il_class, m2m, m2l_leaf, tree_up, tree_m2l, m2l_sector):
    vmem = pl.BlockSpec(memory_space=pltpu.VMEM)
    hbm = pl.BlockSpec(memory_space=pl.ANY)
    block = jax.ShapeDtypeStruct((3, BOXES, SLOTS), F32)
    scratch = [
        pltpu.VMEM((4, COEF, COEF), BF16),
        pltpu.VMEM((4, COEF, COEF), BF16),
        pltpu.VMEM((2, COEF, COEF), BF16),
        pltpu.VMEM((2, COEF, COEF), BF16),
        pltpu.VMEM((15, COEF, COEF), BF16),
        pltpu.VMEM((3, BOXES, SLOTS), F32),
        pltpu.VMEM((3, BOXES, SLOTS), F32),
        pltpu.VMEM((2, 2, 3, BOXES, SLOTS), F32),
        pltpu.VMEM((2, 3, BOXES, SLOTS), F32),
        pltpu.VMEM((2, 2, 8, SLOTS), F32),
        pltpu.VMEM((2, 2, 8, SLOTS), F32),
        pltpu.VMEM((8, CROSS), F32),
        pltpu.VMEM((8, CROSS), F32),
        pltpu.VMEM((5, (BOXES + 1) * 16, SLOTS), F32),
        pltpu.VMEM((5, (BOXES + 1) * 16, SLOTS), F32),
        pltpu.VMEM((BOXES * 16, SLOTS), F32),
        pltpu.VMEM((BOXES * PAD, SLOTS), F32),
        pltpu.VMEM((BOXES * PAD, SLOTS), F32),
        pltpu.VMEM((PAD, CROSS), F32),
        pltpu.VMEM((PAD, CROSS), F32),
        pltpu.VMEM((BOXES, ROWS, SLOTS), BF16),
        pltpu.VMEM((4, BOXES * 8, SLOTS), F32),
        pltpu.VMEM((4, BOXES * 8, SLOTS), F32),
        pltpu.VMEM((BOXES * 8, SLOTS), F32),
        pltpu.VMEM((BOXES * 8, SLOTS), F32),
        pltpu.VMEM((3 * BOXES, ROWS), F32),
        pltpu.VMEM((3 * BOXES, ROWS), BF16),
        pltpu.VMEM((3 * BOXES, ROWS), BF16),
        pltpu.VMEM((ROWS, ROWS), BF16),
        pltpu.VMEM((NCLASS * BOXES, BOXES), BF16),
        pltpu.VMEM((NCLASS, 3 * BOXES, ROWS), BF16),
        pltpu.VMEM((3 * BOXES, ROWS), F32),
        pltpu.VMEM((4, 16, ROWS), F32),
        pltpu.VMEM((4, 8, ROWS), F32),
        pltpu.VMEM((8, ROWS), F32),
        pltpu.VMEM((16, SLOTS), F32),
        pltpu.VMEM((2, 16, SLOTS), BF16),
        pltpu.VMEM((2, GROUP, 16, SLOTS), BF16),
        pltpu.VMEM((32, ROWS), F32),
        pltpu.VMEM((32, ROWS), F32),
        pltpu.VMEM((16, ROWS), F32),
        pltpu.VMEM((48, ROWS), F32),
        pltpu.VMEM((3 * BOXES, ROWS), F32),
        pltpu.VMEM((2, 16, SLOTS), BF16),
        pltpu.VMEM((2, GROUP - 1, 16, SLOTS), BF16),
        pltpu.SemaphoreType.DMA((5,)),
        pltpu.SemaphoreType.DMA((72,)),
        pltpu.SemaphoreType.DMA((72,)),
    ]
    new_places, velocity = pl.pallas_call(
        kernel,
        out_shape=(block, block),
        in_specs=[vmem] * 7 + [hbm] * 5,
        out_specs=(vmem, vmem),
        scratch_shapes=scratch,
        compiler_params=pltpu.CompilerParams(
            collective_id=0, has_side_effects=True, vmem_limit_bytes=52 * 1024 * 1024
        ),
        name="vortex_wake",
    )(
        positions[:, 0], strengths[:, 0], counts, cross_slot, arrive_box, il_source[0], il_class[0],
        m2m, m2l_leaf, tree_up, tree_m2l, m2l_sector,
    )
    return new_places[:, None], velocity[:, None]


def solution(mesh):
    placed = (
        P(None, "sector", "box", None),
        P(None, "sector", "box", None),
        P("sector", "box"),
        P("sector", "box"),
        P("sector", "box"),
        P("sector", "box", None),
        P("sector", "box", None),
        P(),
        P(),
        P(),
        P(),
        P(),
    )
    return jax.shard_map(
        per_device,
        mesh=mesh,
        in_specs=placed,
        out_specs=(P(None, "sector", "box", None), P(None, "sector", "box", None)),
        check_vma=False,
    )
```

time: 379 us -> 173 us (0.46)
  the two profiles are of different devices: /device:TPU:2 before, /device:TPU:1 now
where the time goes in v1:
time: 173 us
  Pallas kernels  163 us (94%)
  local copies, waits for them, and re-layouts  8.96 us (5%)
    pallas_call x1, Pallas kernels, per_device(): pl.pallas_call(kernel, out_shape=(block, block), in_specs=[vmem] * 7 + [h...  163 us
    unnamed x24, local copies, waits for them, and re-layouts  8.96 us

profile of v1, /device:TPU:1, one launch (start us, length us, event | category | flops | bytes accessed | tf_op | source)
XLA Modules:
  0.0 172.6 jit_solution(447791666950614860)
XLA Ops:
  0.6 0.0 copy-start.7
  0.6 0.9 copy.14
  1.5 0.0 copy-start.5
  1.5 0.9 copy.15
  2.4 1.3 copy.18.up_hbm
  3.7 0.0 copy-done.7
  3.7 1.1 copy.19.tm_hbm
  4.8 0.0 copy-done.5
  4.8 0.0 copy-start.6
  4.8 1.6 copy.16.m2m_hbm
  6.4 0.3 copy-done.6
  6.7 0.0 copy-start
  6.7 0.0 copy-start.1
  6.7 0.0 copy-start.2
  6.7 0.0 copy-start.3
  6.8 0.0 copy-start.4
  6.8 1.6 copy.17.m2l_hbm
  8.3 0.0 copy-done
  8.3 0.0 copy-done.1
  8.3 0.0 copy-done.2
  8.3 0.0 copy-done.3
  8.3 0.0 copy-done.4
  8.4 162.9 %vortex_wake.1 = (f32[3,64,128]{2,1,0:T(8,128)S(1)}, f32[3,64,128]{2,1,0:T(8,128)S(1)}) custom-call(f32[3,64,128]{2,1,0:T(8,128)S(1)} %bitcast.12, f32[3,64,128]{2,1,0:T(8,128)S(1)} %bitcast.13, s32[1,64]{1,0:T(1,128)S(1)} %copy-done.4, s32[1,256]{1,0:T(1,128)S(1)} %copy-done.2, s32[1,256]{1,0:T(1,128)S(1)} %copy-done.3, s32[64,16]{1,0:T(8,128)S(1)} %bitcast.10, ...), custom_call_target="tpu_custom_call" | custom-call | tf_op jit(solution)/shard_map/vortex_wake/pallas_call | solution.py:533
  171.3 0.6 copy.24
  171.9 0.6 copy.25
Async XLA Ops:
  0.6 3.1 %copy-start.7 = (bf16[2,441,441]{2,0,1:T(2,128)(2,1)S(1)}, bf16[2,441,441]{2,0,1:T(2,128)(2,1)}, u32[]{:S(2)}) copy-start(bf16[2,441,441]{2,0,1:T(2,128)(2,1)} %param.22) | copy-start | bytes 2333776
  1.5 3.3 %copy-start.5 = (bf16[4,441,441]{2,0,1:T(4,128)(2,1)S(1)}, bf16[4,441,441]{2,0,1:T(4,128)(2,1)}, u32[]{:S(2)}) copy-start(bf16[4,441,441]{2,0,1:T(4,128)(2,1)} %param.19) | copy-start | bytes 4667548
  4.8 1.9 %copy-start.6 = (bf16[4,441,441]{2,0,1:T(4,128)(2,1)S(1)}, bf16[4,441,441]{2,0,1:T(4,128)(2,1)}, u32[]{:S(2)}) copy-start(bf16[4,441,441]{2,0,1:T(4,128)(2,1)} %param.20) | copy-start | bytes 4667548
  6.7 1.6 copy-start
  6.7 1.6 copy-start.1
  6.7 1.6 copy-start.2
  6.7 1.6 copy-start.3
  6.8 1.6 copy-start.4

commit v2 on v1

--- a/solution.py
+++ b/solution.py
@@ -17,6 +17,9 @@
 CROSS = 256
 NCLASS = 4
 GROUP = 16
+LEAF_PER = 8
+NEAR_PER = 8
+FAR_PER = 8
 DELTA_SQ = 0.25
 TIME_STEP = 0.02
 INV_FOUR_PI = 1.0 / (4.0 * math.pi)
@@ -263,7 +266,7 @@
     def box_order(box):
         return (box % 4) * 16 + ((box // 4) % 4) * 4 + box // 16
 
-    def leaf_step(box, carry):
+    def leaf_one(box):
         start = pl.multiple_of(box * PAD, 8)
         b_block = cheb_b[pl.ds(start, PAD), :]
         phi = basis(lambda j: cheb_a[pl.ds(start + j, 1), :], b_block, SLOTS)
@@ -274,7 +277,6 @@
         spot = pl.ds(pl.multiple_of(box_order(box) * 8, 8), 8)
         for t in range(4):
             leaf_box[t, spot, :] = got[:, t * 128 : (t + 1) * 128]
-        return carry
 
     def arrival_terms():
         got_leave.wait_recv()
@@ -368,19 +370,17 @@
             total = part if total is None else total + part
         translated[:, 0:COEF] = total
 
-    def near_step(box, carry):
+    def near_one(box):
         own = pl.ds(pl.multiple_of(box * 16, 16), 16)
         later = pl.ds(pl.multiple_of(box * 16 + 16, 16), 16)
+        spots = [later if kind == 2 else own for kind in range(5)]
         target = tgt_f[own, :].T.astype(BF16)
-        total = jnp.zeros((16, SLOTS), F32)
-        for kind in range(5):
-            spot = later if kind == 2 else own
-            radius_sq = mm(target, src_f[kind, spot, :].astype(BF16))
-            inverse = lax.rsqrt(radius_sq)
-            cubed = (inverse * inverse * inverse).astype(BF16)
-            total = total + mm_t(src_s[kind, spot, :].astype(BF16), cubed)
+        features = jnp.concatenate([src_f[kind, spots[kind], :].astype(BF16) for kind in range(5)], axis=1)
+        sums = jnp.concatenate([src_s[kind, spots[kind], :].astype(BF16) for kind in range(5)], axis=1)
+        inverse = lax.rsqrt(mm(target, features))
+        cubed = (inverse * inverse * inverse).astype(BF16)
+        total = mm_t(sums, cubed)
         near_box[pl.ds(pl.multiple_of(box * 8, 8), 8), :] = total[0:8] + total[8:16]
-        return carry
 
     def downward(local):
         local = local.astype(BF16)
@@ -406,14 +406,21 @@
             for t in range(4):
                 local_box[t, pl.ds(c, BOXES, stride=8), :] = final[c * BOXES : (c + 1) * BOXES, t * 128 : (t + 1) * 128]
 
-    def far_step(box, carry):
+    def far_one(box):
         spot = pl.ds(pl.multiple_of(box_order(box) * 8, 8), 8)
         value = jnp.concatenate([local_box[t, spot, :] for t in range(4)], axis=1)
         high, low = split(value)
         lhs = jnp.concatenate([high, low], axis=0).astype(BF16)
         got = mm(lhs, phi_ref[box])
         far_box[pl.ds(pl.multiple_of(box * 8, 8), 8), :] = got[0:8] + got[8:16]
-        return carry
+
+    def boxes(one, first, last, per):
+        def body(index, carry):
+            for inner in range(per):
+                one(first + index * per + inner)
+            return carry
+
+        lax.fori_loop(0, (last - first) // per, body, 0)
 
     for step in range(2):
         place = pos_ref if step == 0 else places
@@ -421,7 +428,7 @@
             fill_ends(1, places)
             got_halo = send_halo(1, places)
         own_terms(place)
-        lax.fori_loop(0, BOXES, leaf_step, 0)
+        boxes(leaf_one, 0, BOXES, LEAF_PER)
         if step == 0:
             arrival_terms()
             loads[0].wait()
@@ -436,7 +443,7 @@
                 copy.wait()
         translate()
         halo_terms(step)
-        lax.fori_loop(0, BOXES // 2, near_step, 0)
+        boxes(near_one, 0, BOXES // 2, NEAR_PER)
         for copy in got_roots:
             copy.wait_recv()
         top, siblings = tree(step)
@@ -445,7 +452,7 @@
             remote(sec_out.at[step], sec_in.at[step, distance - 1], sector_peer(distance)) for distance in range(1, GROUP)
         ]
         crossed = [mm(siblings[level], tm[bit(level)])[0:4] for level in range(4)]
-        lax.fori_loop(BOXES // 2, BOXES, near_step, 0)
+        boxes(near_one, BOXES // 2, BOXES, NEAR_PER)
         for copy in got_sectors:
             copy.wait_recv()
         total = jnp.zeros((4, COEF), F32)
@@ -456,7 +463,7 @@
         for level in reversed(range(4)):
             local = mm_t(local.astype(BF16), up[bit(level)]) + crossed[level]
         downward(local)
-        lax.fori_loop(0, BOXES, far_step, 0)
+        boxes(far_one, 0, BOXES, FAR_PER)
         near = [near_box[pl.ds(c, BOXES, stride=8), :] for c in range(6)]
         x, y, z = place[0], place[1], place[2]
         swept = (

time: 173 us -> 79.9 us (0.46)
  Pallas kernels: 163 us -> 70 us
    pallas_call x1, Pallas kernels: 163 us -> 70 us  [per_device(): pl.pallas_call(kernel, out_shape=(block, block), in_specs=[vmem] * 7 + [h...]
where the time goes in v2:
time: 79.9 us; the launch traced here: 79.6 us
  Pallas kernels  70 us (88%)
  local copies, waits for them, and re-layouts  8.96 us (11%)
    pallas_call x1, Pallas kernels, per_device(): pl.pallas_call(kernel, out_shape=(block, block), in_specs=[vmem] * 7 + [h...  70 us
    unnamed x24, local copies, waits for them, and re-layouts  8.96 us

profile of v2, /device:TPU:1, one launch (start us, length us, event | category | flops | bytes accessed | tf_op | source)
XLA Modules:
  0.0 79.6 jit_solution(15966935220119521473)
XLA Ops:
  0.6 0.0 copy-start.7
  0.6 0.9 %copy.14 = s32[1,64,16]{2,1,0:T(8,128)S(1)} copy(s32[1,64,16]{1,2,0:T(8,128)} %param.17) | data formatting | bytes 8192 | tf_op args[5]
  1.5 0.0 copy-start.5
  1.5 0.9 %copy.15 = s32[1,64,16]{2,1,0:T(8,128)S(1)} copy(s32[1,64,16]{1,2,0:T(8,128)} %param.18) | data formatting | bytes 8192 | tf_op args[6]
  2.4 1.3 %copy.18.up_hbm = bf16[2,441,441]{2,1,0:T(8,128)(2,1)S(1)} copy(bf16[2,441,441]{2,0,1:T(2,128)(2,1)} %param.21) | data formatting | bytes 1555848 | tf_op args[9]
  3.7 0.0 copy-done.7
  3.7 1.1 %copy.19.tm_hbm = bf16[2,441,441]{2,1,0:T(8,128)(2,1)} copy(bf16[2,441,441]{2,0,1:T(2,128)(2,1)S(1)} %copy-done.7) | data formatting | bytes 1555848 | tf_op args[10]
  4.8 0.0 copy-done.5
  4.8 0.0 copy-start.6
  4.8 1.6 %copy.16.m2m_hbm = bf16[4,441,441]{2,1,0:T(8,128)(2,1)} copy(bf16[4,441,441]{2,0,1:T(4,128)(2,1)S(1)} %copy-done.5) | data formatting | bytes 3111696 | tf_op args[7]
  6.4 0.3 copy-done.6
  6.7 0.0 copy-start
  6.7 0.0 copy-start.1
  6.7 0.0 copy-start.2
  6.7 0.0 copy-start.3
  6.8 0.0 copy-start.4
  6.8 1.6 %copy.17.m2l_hbm = bf16[4,441,441]{2,1,0:T(8,128)(2,1)} copy(bf16[4,441,441]{2,0,1:T(4,128)(2,1)S(1)} %copy-done.6) | data formatting | bytes 3111696 | tf_op args[8]
  8.3 0.0 copy-done
  8.3 0.0 copy-done.1
  8.3 0.0 copy-done.2
  8.3 0.0 copy-done.3
  8.3 0.0 copy-done.4
  8.4 70.0 %vortex_wake.1 = (f32[3,64,128]{2,1,0:T(8,128)S(1)}, f32[3,64,128]{2,1,0:T(8,128)S(1)}) custom-call(f32[3,64,128]{2,1,0:T(8,128)S(1)} %bitcast.12, f32[3,64,128]{2,1,0:T(8,128)S(1)} %bitcast.13, s32[1,64]{1,0:T(1,128)S(1)} %copy-done.4, s32[1,256]{1,0:T(1,128)S(1)} %copy-done.2, s32[1,256]{1,0:T(1,128)S(1)} %copy-done.3, s32[64,16]{1,0:T(8,128)S(1)} %bitcast.10, ...), custom_call_target="tpu_custom_call" | custom-call | tf_op jit(solution)/shard_map/vortex_wake/pallas_call | solution.py:540
  78.4 0.6 copy.24
  79.0 0.6 copy.25
Async XLA Ops:
  0.6 3.1 %copy-start.7 = (bf16[2,441,441]{2,0,1:T(2,128)(2,1)S(1)}, bf16[2,441,441]{2,0,1:T(2,128)(2,1)}, u32[]{:S(2)}) copy-start(bf16[2,441,441]{2,0,1:T(2,128)(2,1)} %param.22) | copy-start | bytes 2333776
  1.5 3.3 %copy-start.5 = (bf16[4,441,441]{2,0,1:T(4,128)(2,1)S(1)}, bf16[4,441,441]{2,0,1:T(4,128)(2,1)}, u32[]{:S(2)}) copy-start(bf16[4,441,441]{2,0,1:T(4,128)(2,1)} %param.19) | copy-start | bytes 4667548
  4.8 1.9 %copy-start.6 = (bf16[4,441,441]{2,0,1:T(4,128)(2,1)S(1)}, bf16[4,441,441]{2,0,1:T(4,128)(2,1)}, u32[]{:S(2)}) copy-start(bf16[4,441,441]{2,0,1:T(4,128)(2,1)} %param.20) | copy-start | bytes 4667548
  6.7 1.6 %copy-start = (f32[3,1,64,128]{3,2,1,0:T(8,128)S(1)}, f32[3,1,64,128]{3,2,1,0:T(8,128)}, u32[]{:S(2)}) copy-start(f32[3,1,64,128]{3,2,1,0:T(8,128)} %param.12) | copy-start | bytes 294916
  6.7 1.6 %copy-start.1 = (f32[3,1,64,128]{3,2,1,0:T(8,128)S(1)}, f32[3,1,64,128]{3,2,1,0:T(8,128)}, u32[]{:S(2)}) copy-start(f32[3,1,64,128]{3,2,1,0:T(8,128)} %param.13) | copy-start | bytes 294916
  6.7 1.6 %copy-start.2 = (s32[1,256]{1,0:T(1,128)S(1)}, s32[1,256]{1,0:T(1,128)}, u32[]{:S(2)}) copy-start(s32[1,256]{1,0:T(1,128)} %cross_ref.1) | copy-start | bytes 3076
  6.7 1.6 %copy-start.3 = (s32[1,256]{1,0:T(1,128)S(1)}, s32[1,256]{1,0:T(1,128)}, u32[]{:S(2)}) copy-start(s32[1,256]{1,0:T(1,128)} %arr_ref.1) | copy-start | bytes 3076
  6.8 1.6 %copy-start.4 = (s32[1,64]{1,0:T(1,128)S(1)}, s32[1,64]{1,0:T(1,128)}, u32[]{:S(2)}) copy-start(s32[1,64]{1,0:T(1,128)} %cnt_ref.1) | copy-start | bytes 772

commit v3 on v2

--- a/solution.py
+++ b/solution.py
@@ -17,9 +17,11 @@
 CROSS = 256
 NCLASS = 4
 GROUP = 16
-LEAF_PER = 8
-NEAR_PER = 8
-FAR_PER = 8
+LEAF_PER = 16
+WAIT_A = 0
+TREE_END = 16
+WAIT_B = 24
+FAR_PER = 16
 DELTA_SQ = 0.25
 TIME_STEP = 0.02
 INV_FOUR_PI = 1.0 / (4.0 * math.pi)
@@ -67,6 +69,7 @@
     arr_leaf, leaf504, leaf441, select, counts_pc, presum, translated,
     up1, up2, root, pack_f, root_out, root_in, tree_e, tree_o, down1, down2, down3,
     sec_out, sec_in,
+    m2m_t, up_t, select_t, sec_rows,
     load_sem, send_sem, recv_sem,
 ):
     s_id = lax.axis_index("sector")
@@ -159,11 +162,14 @@
     row = iota((ROWS, ROWS), 0)
     order = (row * 2731) >> 16
     select[...] = one_where((iota((ROWS, ROWS), 1) == row - 3 * order) & (row - PAD * order < TERMS) & (order < TERMS), BF16)
+    wide = iota((COEF, ROWS), 1)
+    group = (wide * 2731) >> 16
+    select_t[...] = one_where((iota((COEF, ROWS), 0) == wide - 3 * group) & (wide - PAD * group < TERMS) & (group < TERMS), BF16)
     for ref in (cheb_a, cheb_b, arr_a, arr_b, up1, up2, root, pack_f, tree_e, tree_o, down1, down2, local_box):
         ref[...] = jnp.zeros_like(ref)
 
     permute = one_where(reversed_digits(iota((BOXES, BOXES), 0)) == iota((BOXES, BOXES), 1), BF16)
-    code = mm(permute, (ils_ref[...] + BOXES * ilc_ref[...]).astype(F32).astype(BF16))
+    code = mm_t(permute, (ils_ref[...] + BOXES * ilc_ref[...]).astype(F32).astype(BF16))
     source = reversed_digits(iota((BOXES, BOXES), 1)).astype(F32)
     for kind in range(NCLASS):
         wanted = source + float(BOXES * kind)
@@ -187,7 +193,7 @@
         for index, value in enumerate(rows):
             tgt_f[pl.ds(index, BOXES, stride=16), :] = value
 
-    def put_sources(kind, base, count, coords, weight):
+    def put_sources(kind, base, count, coords, weight, first):
         offset = OFFSETS[kind]
         x, y, z = (v + o if o else v for v, o in zip(coords, offset))
         halves = [split(-2.0 * v) for v in (x, y, z)]
@@ -202,12 +208,16 @@
         zero = jnp.zeros_like(x)
         sums = [h for h, _ in parts] + [zero] * 2 + [l for _, l in parts] + [zero] * 2
         for index in range(16):
+            fixed_f = index in (9, 10, 11, 15)
+            fixed_s = index % 8 not in (3, 4, 5)
             if count == 1:
                 spot = slice(base * 16 + index, base * 16 + index + 1)
             else:
                 spot = pl.ds(base * 16 + index, count, stride=16)
-            src_f[kind, spot, :] = rows[index]
-            src_s[kind, spot, :] = sums[index]
+            if first or not fixed_f:
+                src_f[kind, spot, :] = rows[index]
+            if first or not fixed_s:
+                src_s[kind, spot, :] = sums[index]
 
     for index in range(12, 16):
         tgt_f[pl.ds(index, BOXES, stride=16), :] = jnp.full((BOXES, SLOTS), 1.0 if index < 15 else 0.0, F32)
@@ -221,13 +231,13 @@
             older, newer = newer, 2.0 * scaled * newer - older
             put(index, newer)
 
-    def own_terms(place):
+    def own_terms(step, place):
         x, y, z = place[0], place[1], place[2]
         weight = (weights[0], weights[1], weights[2])
         put_targets(x, y, z)
-        put_sources(0, 0, BOXES, (x, y, z), weight)
-        put_sources(1, 1, BOXES, (x, y, z), weight)
-        put_sources(2, 0, BOXES, (x, y, z), weight)
+        put_sources(0, 0, BOXES, (x, y, z), weight, step == 0)
+        put_sources(1, 1, BOXES, (x, y, z), weight, step == 0)
+        put_sources(2, 0, BOXES, (x, y, z), weight, step == 0)
 
         def put_a(index, value):
             cheb_a[pl.ds(index, BOXES, stride=PAD), :] = value
@@ -245,14 +255,14 @@
                 got_weights[side].wait_recv()
             coords = tuple(halo_p[step, side, c] for c in range(3))
             weight = tuple(halo_w[side, c] for c in range(3))
-            put_sources(3 + side, 0, BOXES, coords, weight)
+            put_sources(3 + side, 0, BOXES, coords, weight, step == 0)
         for side in range(2):
             got_halo[2 + side].wait_recv()
             inside = (g_id > 0) if side == 0 else (g_id < GROUP - 1)
             keep = jnp.where(inside, 1.0, 0.0).astype(F32)
             coords = tuple(end_in[step, side, c : c + 1, :] for c in range(3))
             weight = tuple(end_in[step, side, 3 + c : 4 + c, :] * keep for c in range(3))
-            put_sources(1 + side, 0 if side == 0 else BOXES, 1, coords, weight)
+            put_sources(1 + side, 0 if side == 0 else BOXES, 1, coords, weight, step == 0)
 
     def basis(a_row, b_block, width):
         pieces = []
@@ -353,6 +363,7 @@
         for level in range(4):
             siblings.append(upper[0:8] if upper.shape[0] >= 8 else upper)
             merged = mm(lower, up[bit(level)]) + mm(upper, up[1 - bit(level)])
+            yield
             if level < 3:
                 half = merged.shape[0] // 2
                 lower = merged[0:half].astype(BF16)
@@ -385,26 +396,61 @@
     def downward(local):
         local = local.astype(BF16)
         for o in range(4):
-            part = rounded(mm_t(local, m2m[o]))
+            part = rounded(mm(local, m2m_t[o]))
             for c in range(3):
                 down1[c * 4 + o : c * 4 + o + 1, 0:COEF] = part[c : c + 1]
+            yield
         level = down1[:, 0:COEF].astype(BF16)
         for o in range(4):
-            part = rounded(mm_t(level, m2m[o]))
+            part = rounded(mm(level, m2m_t[o]))
             for c in range(3):
                 down2[c * 16 + o * 4 : c * 16 + o * 4 + 4, 0:COEF] = part[c * 4 : c * 4 + 4]
+            yield
         level = down2[:, 0:COEF].astype(BF16)
         for o in range(4):
-            part = mm_t(level, m2m[o])
+            part = mm(level, m2m_t[o])
             for c in range(3):
                 rows = slice(c * BOXES + o * 16, c * BOXES + o * 16 + 16)
                 down3[rows, 0:COEF] = part[c * 16 : c * 16 + 16] + translated[rows, 0:COEF]
-        high, low = split(down3[:, 0:COEF])
-        chosen = select[:, 0:COEF]
-        final = mm_t(high.astype(BF16), chosen) + mm_t(low.astype(BF16), chosen)
+            yield
         for c in range(3):
+            high, low = split(down3[c * BOXES : (c + 1) * BOXES, 0:COEF])
+            final = mm(high.astype(BF16), select_t[...]) + mm(low.astype(BF16), select_t[...])
             for t in range(4):
-                local_box[t, pl.ds(c, BOXES, stride=8), :] = final[c * BOXES : (c + 1) * BOXES, t * 128 : (t + 1) * 128]
+                local_box[t, pl.ds(c, BOXES, stride=8), :] = final[:, t * 128 : (t + 1) * 128]
+            yield
+
+    def last_chain(step, crossed):
+        total = jnp.zeros((4, COEF), F32)
+        for distance in range(1, GROUP):
+            spread(distance - 1, sec_in.at[step], (sec_rows.at[distance - 1], 0))
+            total = total + mm(sec_rows[distance - 1, 0:4, 0:COEF].astype(BF16), sec[GROUP - 1 - distance])
+            if distance % 4 == 0:
+                yield
+        local = total
+        for level in reversed(range(4)):
+            local = mm(local.astype(BF16), up_t[bit(level)]) + crossed[level]
+            yield
+        yield from downward(local)
+
+    def interleave(chain, first, last, steps):
+        done, result = 0, None
+        while True:
+            try:
+                next(chain)
+            except StopIteration as stop:
+                result = stop.value
+                break
+            done += 1
+            until = min(last, first + -(-(last - first) * done // steps)) if steps else first
+            for box in range(interleave_at[0], until):
+                near_one(box)
+            interleave_at[0] = max(interleave_at[0], until)
+        for box in range(interleave_at[0], last):
+            near_one(box)
+        return result
+
+    interleave_at = [0]
 
     def far_one(box):
         spot = pl.ds(pl.multiple_of(box_order(box) * 8, 8), 8)
@@ -427,7 +473,7 @@
         if step == 1:
             fill_ends(1, places)
             got_halo = send_halo(1, places)
-        own_terms(place)
+        own_terms(step, place)
         boxes(leaf_one, 0, BOXES, LEAF_PER)
         if step == 0:
             arrival_terms()
@@ -441,28 +487,29 @@
         if step == 0:
             for copy in loads[1:]:
                 copy.wait()
+            for index in range(4):
+                m2m_t[index] = m2m[index].T
+            for index in range(2):
+                up_t[index] = up[index].T
         translate()
         halo_terms(step)
-        boxes(near_one, 0, BOXES // 2, NEAR_PER)
+        for box in range(0, WAIT_A):
+            near_one(box)
         for copy in got_roots:
             copy.wait_recv()
-        top, siblings = tree(step)
+        interleave_at[0] = WAIT_A
+        top, siblings = interleave(tree(step), WAIT_A, TREE_END, 4)
         pack(jnp.concatenate([top, jnp.zeros((4, COEF), F32)], axis=0), sec_out.at[step])
         got_sectors = [
             remote(sec_out.at[step], sec_in.at[step, distance - 1], sector_peer(distance)) for distance in range(1, GROUP)
         ]
         crossed = [mm(siblings[level], tm[bit(level)])[0:4] for level in range(4)]
-        boxes(near_one, BOXES // 2, BOXES, NEAR_PER)
+        for box in range(TREE_END, WAIT_B):
+            near_one(box)
         for copy in got_sectors:
             copy.wait_recv()
-        total = jnp.zeros((4, COEF), F32)
-        for distance in range(1, GROUP):
-            spread(distance - 1, sec_in.at[step], (root, 0))
-            total = total + mm(root[0:4, 0:COEF].astype(BF16), sec[GROUP - 1 - distance])
-        local = total
-        for level in reversed(range(4)):
-            local = mm_t(local.astype(BF16), up[bit(level)]) + crossed[level]
-        downward(local)
+        interleave_at[0] = WAIT_B
+        interleave(last_chain(step, crossed), WAIT_B, BOXES, 22)
         boxes(far_one, 0, BOXES, FAR_PER)
         near = [near_box[pl.ds(c, BOXES, stride=8), :] for c in range(6)]
         x, y, z = place[0], place[1], place[2]
@@ -533,6 +580,10 @@
         pltpu.VMEM((3 * BOXES, ROWS), F32),
         pltpu.VMEM((2, 16, SLOTS), BF16),
         pltpu.VMEM((2, GROUP - 1, 16, SLOTS), BF16),
+        pltpu.VMEM((4, COEF, COEF), BF16),
+        pltpu.VMEM((2, COEF, COEF), BF16),
+        pltpu.VMEM((COEF, ROWS), BF16),
+        pltpu.VMEM((GROUP - 1, 8, ROWS), F32),
         pltpu.SemaphoreType.DMA((5,)),
         pltpu.SemaphoreType.DMA((72,)),
         pltpu.SemaphoreType.DMA((72,)),
@@ -548,7 +599,7 @@
         ),
         name="vortex_wake",
     )(
-        positions[:, 0], strengths[:, 0], counts, cross_slot, arrive_box, il_source[0], il_class[0],
+        positions[:, 0], strengths[:, 0], counts, cross_slot, arrive_box, il_source[0].T, il_class[0].T,
         m2m, m2l_leaf, tree_up, tree_m2l, m2l_sector,
     )
     return new_places[:, None], velocity[:, None]

time: 79.9 us -> 78.2 us (0.979)
  local copies, waits for them, and re-layouts: 8.96 us -> 7.39 us
    unnamed x24 -> x26, local copies, waits for them, and re-layouts: 8.96 us -> 7.39 us
where the time goes in v3:
time: 78.2 us; the launch traced here: 78.1 us
  Pallas kernels  69.9 us (89%)
  local copies, waits for them, and re-layouts  7.39 us (9%)
    pallas_call x1, Pallas kernels, per_device(): pl.pallas_call(kernel, out_shape=(block, block), in_specs=[vmem] * 7 + [h...  69.9 us
    unnamed x26, local copies, waits for them, and re-layouts  7.39 us

profile of v3, /device:TPU:1, one launch (start us, length us, event | category | flops | bytes accessed | tf_op | source)
XLA Modules:
  0.0 78.1 jit_solution(18265748821623628478)
XLA Ops:
  0.6 0.0 copy-start.9
  0.6 0.0 copy-start.7
  0.7 1.5 %copy.16.up_hbm = bf16[2,441,441]{2,1,0:T(8,128)(2,1)S(1)} copy(bf16[2,441,441]{2,0,1:T(2,128)(2,1)} %param.21) | data formatting | bytes 1555848 | tf_op args[9]
  2.1 0.0 copy-done.9
  2.1 1.1 %copy.17.tm_hbm = bf16[2,441,441]{2,1,0:T(8,128)(2,1)} copy(bf16[2,441,441]{2,0,1:T(2,128)(2,1)S(1)} %copy-done.9) | data formatting | bytes 1555848 | tf_op args[10]
  3.2 0.0 copy-done.7
  3.2 0.0 copy-start.8
  3.2 1.6 %copy.14.m2m_hbm = bf16[4,441,441]{2,1,0:T(8,128)(2,1)} copy(bf16[4,441,441]{2,0,1:T(4,128)(2,1)S(1)} %copy-done.7) | data formatting | bytes 3111696 | tf_op args[7]
  4.8 0.3 copy-done.8
  5.1 0.0 copy-start
  5.1 0.0 copy-start.1
  5.1 0.0 copy-start.2
  5.1 0.0 copy-start.3
  5.1 0.0 copy-start.4
  5.2 0.0 copy-start.5
  5.2 0.0 copy-start.6
  5.2 1.6 %copy.15.m2l_hbm = bf16[4,441,441]{2,1,0:T(8,128)(2,1)} copy(bf16[4,441,441]{2,0,1:T(4,128)(2,1)S(1)} %copy-done.8) | data formatting | bytes 3111696 | tf_op args[8]
  6.8 0.0 copy-done
  6.8 0.0 copy-done.1
  6.8 0.0 copy-done.2
  6.8 0.0 copy-done.3
  6.8 0.0 copy-done.4
  6.8 0.0 copy-done.5
  6.8 0.0 copy-done.6
  6.8 69.9 %vortex_wake.1 = (f32[3,64,128]{2,1,0:T(8,128)S(1)}, f32[3,64,128]{2,1,0:T(8,128)S(1)}) custom-call(f32[3,64,128]{2,1,0:T(8,128)S(1)} %bitcast.14, f32[3,64,128]{2,1,0:T(8,128)S(1)} %bitcast.15, s32[1,64]{1,0:T(1,128)S(1)} %copy-done.6, s32[1,256]{1,0:T(1,128)S(1)} %copy-done.4, s32[1,256]{1,0:T(1,128)S(1)} %copy-done.5, s32[16,64]{1,0:T(8,128)S(1)} %bitcast.18, ...), custom_call_target="tpu_custom_call" | custom-call | tf_op jit(solution)/shard_map/vortex_wake/pallas_call | solution.py:591
  76.8 0.6 copy.22
  77.4 0.6 copy.23
Async XLA Ops:
  0.6 1.5 %copy-start.9 = (bf16[2,441,441]{2,0,1:T(2,128)(2,1)S(1)}, bf16[2,441,441]{2,0,1:T(2,128)(2,1)}, u32[]{:S(2)}) copy-start(bf16[2,441,441]{2,0,1:T(2,128)(2,1)} %param.22) | copy-start | bytes 2333776
  0.6 2.6 %copy-start.7 = (bf16[4,441,441]{2,0,1:T(4,128)(2,1)S(1)}, bf16[4,441,441]{2,0,1:T(4,128)(2,1)}, u32[]{:S(2)}) copy-start(bf16[4,441,441]{2,0,1:T(4,128)(2,1)} %param.19) | copy-start | bytes 4667548
  3.2 1.9 %copy-start.8 = (bf16[4,441,441]{2,0,1:T(4,128)(2,1)S(1)}, bf16[4,441,441]{2,0,1:T(4,128)(2,1)}, u32[]{:S(2)}) copy-start(bf16[4,441,441]{2,0,1:T(4,128)(2,1)} %param.20) | copy-start | bytes 4667548
  5.1 1.6 %copy-start = (f32[3,1,64,128]{3,2,1,0:T(8,128)S(1)}, f32[3,1,64,128]{3,2,1,0:T(8,128)}, u32[]{:S(2)}) copy-start(f32[3,1,64,128]{3,2,1,0:T(8,128)} %param.12) | copy-start | bytes 294916
  5.1 1.6 %copy-start.1 = (f32[3,1,64,128]{3,2,1,0:T(8,128)S(1)}, f32[3,1,64,128]{3,2,1,0:T(8,128)}, u32[]{:S(2)}) copy-start(f32[3,1,64,128]{3,2,1,0:T(8,128)} %param.13) | copy-start | bytes 294916
  5.1 1.6 %copy-start.2 = (s32[1,64,16]{1,2,0:T(8,128)S(1)}, s32[1,64,16]{1,2,0:T(8,128)}, u32[]{:S(2)}) copy-start(s32[1,64,16]{1,2,0:T(8,128)} %param.17) | copy-start | bytes 12292
  5.1 1.6 %copy-start.3 = (s32[1,64,16]{1,2,0:T(8,128)S(1)}, s32[1,64,16]{1,2,0:T(8,128)}, u32[]{:S(2)}) copy-start(s32[1,64,16]{1,2,0:T(8,128)} %param.18) | copy-start | bytes 12292
  5.1 1.6 %copy-start.4 = (s32[1,256]{1,0:T(1,128)S(1)}, s32[1,256]{1,0:T(1,128)}, u32[]{:S(2)}) copy-start(s32[1,256]{1,0:T(1,128)} %cross_ref.1) | copy-start | bytes 3076
  5.2 1.6 %copy-start.5 = (s32[1,256]{1,0:T(1,128)S(1)}, s32[1,256]{1,0:T(1,128)}, u32[]{:S(2)}) copy-start(s32[1,256]{1,0:T(1,128)} %arr_ref.1) | copy-start | bytes 3076
  5.2 1.6 %copy-start.6 = (s32[1,64]{1,0:T(1,128)S(1)}, s32[1,64]{1,0:T(1,128)}, u32[]{:S(2)}) copy-start(s32[1,64]{1,0:T(1,128)} %cnt_ref.1) | copy-start | bytes 772

commit v4 on v3

--- a/solution.py
+++ b/solution.py
@@ -17,10 +17,13 @@
 CROSS = 256
 NCLASS = 4
 GROUP = 16
+BOX_ORDER = (8, 9, 10, 11, 6, 7, 14, 15, 12, 13, 4, 5, 2, 3, 1)
+SECTOR_ORDER = (10, 9, 11, 6, 14, 5, 7, 13, 15, 8, 2, 3, 1, 4, 12)
 LEAF_PER = 16
-WAIT_A = 0
-TREE_END = 16
-WAIT_B = 24
+NEAR_PER = 8
+WAIT_A = 16
+TREE_END = 20
+WAIT_B = 44
 FAR_PER = 16
 DELTA_SQ = 0.25
 TIME_STEP = 0.02
@@ -93,8 +96,8 @@
 
     barrier = pltpu.get_barrier_semaphore()
     for distance in range(1, GROUP):
-        pl.semaphore_signal(barrier, inc=1, device_id=box_peer(distance), device_id_type=MESH)
-        pl.semaphore_signal(barrier, inc=1, device_id=sector_peer(distance), device_id_type=MESH)
+        pl.semaphore_signal(barrier, inc=1, device_id=box_peer(BOX_ORDER[distance - 1]), device_id_type=MESH)
+        pl.semaphore_signal(barrier, inc=1, device_id=sector_peer(SECTOR_ORDER[distance - 1]), device_id_type=MESH)
     before = (s_id, (g_id + GROUP - 1) % GROUP)
     after = (s_id, (g_id + 1) % GROUP)
 
@@ -141,10 +144,6 @@
             end_out[step, 0, 3 + c : 4 + c, :] = weights[c, BOXES - 1 : BOXES, :]
             end_out[step, 1, 3 + c : 4 + c, :] = weights[c, 0:1, :]
 
-    fill_ends(0, pos_ref)
-    pl.semaphore_wait(barrier, 2 * (GROUP - 1))
-    got_leave = remote(leave_out, leave_in, sector_peer(1))
-
     def send_halo(step, place):
         return [
             remote(place, halo_p.at[step, 0], sector_peer(1)),
@@ -152,12 +151,6 @@
             remote(end_out.at[step, 0], end_in.at[step, 0], after),
             remote(end_out.at[step, 1], end_in.at[step, 1], before),
         ]
-
-    got_weights = [
-        remote(weights, halo_w.at[0], sector_peer(1)),
-        remote(weights, halo_w.at[1], sector_peer(GROUP - 1)),
-    ]
-    got_halo = send_halo(0, pos_ref)
 
     row = iota((ROWS, ROWS), 0)
     order = (row * 2731) >> 16
@@ -468,12 +461,22 @@
 
         lax.fori_loop(0, (last - first) // per, body, 0)
 
+    fill_ends(0, pos_ref)
+    own_terms(0, pos_ref)
+    pl.semaphore_wait(barrier, 2 * (GROUP - 1))
+    got_leave = remote(leave_out, leave_in, sector_peer(1))
+    got_weights = [
+        remote(weights, halo_w.at[0], sector_peer(1)),
+        remote(weights, halo_w.at[1], sector_peer(GROUP - 1)),
+    ]
+    got_halo = send_halo(0, pos_ref)
+
     for step in range(2):
         place = pos_ref if step == 0 else places
         if step == 1:
             fill_ends(1, places)
             got_halo = send_halo(1, places)
-        own_terms(step, place)
+            own_terms(1, places)
         boxes(leaf_one, 0, BOXES, LEAF_PER)
         if step == 0:
             arrival_terms()
@@ -482,7 +485,7 @@
         pack(upward(), root_out.at[step])
         root_in[step, 0] = root_out[step]
         got_roots = [
-            remote(root_out.at[step], root_in.at[step, distance], box_peer(distance)) for distance in range(1, GROUP)
+            remote(root_out.at[step], root_in.at[step, distance], box_peer(distance)) for distance in BOX_ORDER
         ]
         if step == 0:
             for copy in loads[1:]:
@@ -493,19 +496,17 @@
                 up_t[index] = up[index].T
         translate()
         halo_terms(step)
-        for box in range(0, WAIT_A):
-            near_one(box)
+        boxes(near_one, 0, WAIT_A, NEAR_PER)
         for copy in got_roots:
             copy.wait_recv()
         interleave_at[0] = WAIT_A
         top, siblings = interleave(tree(step), WAIT_A, TREE_END, 4)
         pack(jnp.concatenate([top, jnp.zeros((4, COEF), F32)], axis=0), sec_out.at[step])
         got_sectors = [
-            remote(sec_out.at[step], sec_in.at[step, distance - 1], sector_peer(distance)) for distance in range(1, GROUP)
+            remote(sec_out.at[step], sec_in.at[step, distance - 1], sector_peer(distance)) for distance in SECTOR_ORDER
         ]
         crossed = [mm(siblings[level], tm[bit(level)])[0:4] for level in range(4)]
-        for box in range(TREE_END, WAIT_B):
-            near_one(box)
+        boxes(near_one, TREE_END, WAIT_B, NEAR_PER)
         for copy in got_sectors:
             copy.wait_recv()
         interleave_at[0] = WAIT_B

time: 78.2 us -> 71.6 us (0.916)
  Pallas kernels: 69.9 us -> 63.3 us
    pallas_call x1, Pallas kernels: 69.9 us -> 63.3 us  [per_device(): pl.pallas_call(kernel, out_shape=(block, block), in_specs=[vmem] * 7 + [h...]
where the time goes in v4:
time: 71.6 us; the launch traced here: 71.5 us
  Pallas kernels  63.3 us (88%)
  local copies, waits for them, and re-layouts  7.39 us (10%)
  between operations  0.73 us (1%)
    pallas_call x1, Pallas kernels, per_device(): pl.pallas_call(kernel, out_shape=(block, block), in_specs=[vmem] * 7 + [h...  63.3 us
    unnamed x26, local copies, waits for them, and re-layouts  7.39 us

profile of v4, /device:TPU:1, one launch (start us, length us, event | category | flops | bytes accessed | tf_op | source)
XLA Modules:
  0.0 71.5 jit_solution(935685056357029875)
XLA Ops:
  0.6 0.0 copy-start.9
  0.6 0.0 copy-start.7
  0.7 1.5 %copy.16.up_hbm = bf16[2,441,441]{2,1,0:T(8,128)(2,1)S(1)} copy(bf16[2,441,441]{2,0,1:T(2,128)(2,1)} %param.21) | data formatting | bytes 1555848 | tf_op args[9]
  2.1 0.0 copy-done.9
  2.1 1.1 %copy.17.tm_hbm = bf16[2,441,441]{2,1,0:T(8,128)(2,1)} copy(bf16[2,441,441]{2,0,1:T(2,128)(2,1)S(1)} %copy-done.9) | data formatting | bytes 1555848 | tf_op args[10]
  3.2 0.0 copy-done.7
  3.2 0.0 copy-start.8
  3.2 1.6 %copy.14.m2m_hbm = bf16[4,441,441]{2,1,0:T(8,128)(2,1)} copy(bf16[4,441,441]{2,0,1:T(4,128)(2,1)S(1)} %copy-done.7) | data formatting | bytes 3111696 | tf_op args[7]
  4.8 0.3 copy-done.8
  5.1 0.0 copy-start
  5.1 0.0 copy-start.1
  5.1 0.0 copy-start.2
  5.1 0.0 copy-start.3
  5.1 0.0 copy-start.4
  5.2 0.0 copy-start.5
  5.2 0.0 copy-start.6
  5.2 1.6 %copy.15.m2l_hbm = bf16[4,441,441]{2,1,0:T(8,128)(2,1)} copy(bf16[4,441,441]{2,0,1:T(4,128)(2,1)S(1)} %copy-done.8) | data formatting | bytes 3111696 | tf_op args[8]
  6.8 0.0 copy-done
  6.8 0.0 copy-done.1
  6.8 0.0 copy-done.2
  6.8 0.0 copy-done.3
  6.8 0.0 copy-done.4
  6.8 0.0 copy-done.5
  6.8 0.0 copy-done.6
  6.8 63.3 %vortex_wake.1 = (f32[3,64,128]{2,1,0:T(8,128)S(1)}, f32[3,64,128]{2,1,0:T(8,128)S(1)}) custom-call(f32[3,64,128]{2,1,0:T(8,128)S(1)} %bitcast.14, f32[3,64,128]{2,1,0:T(8,128)S(1)} %bitcast.15, s32[1,64]{1,0:T(1,128)S(1)} %copy-done.6, s32[1,256]{1,0:T(1,128)S(1)} %copy-done.4, s32[1,256]{1,0:T(1,128)S(1)} %copy-done.5, s32[16,64]{1,0:T(8,128)S(1)} %bitcast.18, ...), custom_call_target="tpu_custom_call" | custom-call | tf_op jit(solution)/shard_map/vortex_wake/pallas_call | solution.py:592
  70.2 0.6 copy.22
  70.8 0.6 copy.23
Async XLA Ops:
  0.6 1.5 %copy-start.9 = (bf16[2,441,441]{2,0,1:T(2,128)(2,1)S(1)}, bf16[2,441,441]{2,0,1:T(2,128)(2,1)}, u32[]{:S(2)}) copy-start(bf16[2,441,441]{2,0,1:T(2,128)(2,1)} %param.22) | copy-start | bytes 2333776
  0.6 2.6 %copy-start.7 = (bf16[4,441,441]{2,0,1:T(4,128)(2,1)S(1)}, bf16[4,441,441]{2,0,1:T(4,128)(2,1)}, u32[]{:S(2)}) copy-start(bf16[4,441,441]{2,0,1:T(4,128)(2,1)} %param.19) | copy-start | bytes 4667548
  3.2 1.9 %copy-start.8 = (bf16[4,441,441]{2,0,1:T(4,128)(2,1)S(1)}, bf16[4,441,441]{2,0,1:T(4,128)(2,1)}, u32[]{:S(2)}) copy-start(bf16[4,441,441]{2,0,1:T(4,128)(2,1)} %param.20) | copy-start | bytes 4667548
  5.1 1.6 %copy-start = (f32[3,1,64,128]{3,2,1,0:T(8,128)S(1)}, f32[3,1,64,128]{3,2,1,0:T(8,128)}, u32[]{:S(2)}) copy-start(f32[3,1,64,128]{3,2,1,0:T(8,128)} %param.12) | copy-start | bytes 294916
  5.1 1.6 %copy-start.1 = (f32[3,1,64,128]{3,2,1,0:T(8,128)S(1)}, f32[3,1,64,128]{3,2,1,0:T(8,128)}, u32[]{:S(2)}) copy-start(f32[3,1,64,128]{3,2,1,0:T(8,128)} %param.13) | copy-start | bytes 294916
  5.1 1.6 %copy-start.2 = (s32[1,64,16]{1,2,0:T(8,128)S(1)}, s32[1,64,16]{1,2,0:T(8,128)}, u32[]{:S(2)}) copy-start(s32[1,64,16]{1,2,0:T(8,128)} %param.17) | copy-start | bytes 12292
  5.1 1.6 %copy-start.3 = (s32[1,64,16]{1,2,0:T(8,128)S(1)}, s32[1,64,16]{1,2,0:T(8,128)}, u32[]{:S(2)}) copy-start(s32[1,64,16]{1,2,0:T(8,128)} %param.18) | copy-start | bytes 12292
  5.1 1.6 %copy-start.4 = (s32[1,256]{1,0:T(1,128)S(1)}, s32[1,256]{1,0:T(1,128)}, u32[]{:S(2)}) copy-start(s32[1,256]{1,0:T(1,128)} %cross_ref.1) | copy-start | bytes 3076
  5.2 1.6 %copy-start.5 = (s32[1,256]{1,0:T(1,128)S(1)}, s32[1,256]{1,0:T(1,128)}, u32[]{:S(2)}) copy-start(s32[1,256]{1,0:T(1,128)} %arr_ref.1) | copy-start | bytes 3076
  5.2 1.6 %copy-start.6 = (s32[1,64]{1,0:T(1,128)S(1)}, s32[1,64]{1,0:T(1,128)}, u32[]{:S(2)}) copy-start(s32[1,64]{1,0:T(1,128)} %cnt_ref.1) | copy-start | bytes 772

commit v5 on v4

--- a/solution.py
+++ b/solution.py
@@ -21,9 +21,7 @@
 SECTOR_ORDER = (10, 9, 11, 6, 14, 5, 7, 13, 15, 8, 2, 3, 1, 4, 12)
 LEAF_PER = 16
 NEAR_PER = 8
-WAIT_A = 16
-TREE_END = 20
-WAIT_B = 44
+SPLITS = ((16, 20, 44), (12, 16, 40))
 FAR_PER = 16
 DELTA_SQ = 0.25
 TIME_STEP = 0.02
@@ -232,14 +230,15 @@
         put_sources(1, 1, BOXES, (x, y, z), weight, step == 0)
         put_sources(2, 0, BOXES, (x, y, z), weight, step == 0)
 
+    def own_series(place):
         def put_a(index, value):
             cheb_a[pl.ds(index, BOXES, stride=PAD), :] = value
 
         def put_b(index, value):
             cheb_b[pl.ds(index, BOXES, stride=PAD), :] = value
 
-        series(x, put_a)
-        series(y, put_b)
+        series(place[0], put_a)
+        series(place[1], put_b)
 
     def halo_terms(step):
         for side in range(2):
@@ -463,6 +462,7 @@
 
     fill_ends(0, pos_ref)
     own_terms(0, pos_ref)
+    own_series(pos_ref)
     pl.semaphore_wait(barrier, 2 * (GROUP - 1))
     got_leave = remote(leave_out, leave_in, sector_peer(1))
     got_weights = [
@@ -476,7 +476,7 @@
         if step == 1:
             fill_ends(1, places)
             got_halo = send_halo(1, places)
-            own_terms(1, places)
+            own_series(places)
         boxes(leaf_one, 0, BOXES, LEAF_PER)
         if step == 0:
             arrival_terms()
@@ -494,23 +494,26 @@
                 m2m_t[index] = m2m[index].T
             for index in range(2):
                 up_t[index] = up[index].T
+        else:
+            own_terms(1, places)
         translate()
         halo_terms(step)
-        boxes(near_one, 0, WAIT_A, NEAR_PER)
+        wait_a, tree_end, wait_b = SPLITS[step]
+        boxes(near_one, 0, wait_a, NEAR_PER if wait_a % NEAR_PER == 0 else wait_a)
         for copy in got_roots:
             copy.wait_recv()
-        interleave_at[0] = WAIT_A
-        top, siblings = interleave(tree(step), WAIT_A, TREE_END, 4)
+        interleave_at[0] = wait_a
+        top, siblings = interleave(tree(step), wait_a, tree_end, 4)
         pack(jnp.concatenate([top, jnp.zeros((4, COEF), F32)], axis=0), sec_out.at[step])
         got_sectors = [
             remote(sec_out.at[step], sec_in.at[step, distance - 1], sector_peer(distance)) for distance in SECTOR_ORDER
         ]
         crossed = [mm(siblings[level], tm[bit(level)])[0:4] for level in range(4)]
-        boxes(near_one, TREE_END, WAIT_B, NEAR_PER)
+        boxes(near_one, tree_end, wait_b, NEAR_PER)
         for copy in got_sectors:
             copy.wait_recv()
-        interleave_at[0] = WAIT_B
-        interleave(last_chain(step, crossed), WAIT_B, BOXES, 22)
+        interleave_at[0] = wait_b
+        interleave(last_chain(step, crossed), wait_b, BOXES, 22)
         boxes(far_one, 0, BOXES, FAR_PER)
         near = [near_box[pl.ds(c, BOXES, stride=8), :] for c in range(6)]
         x, y, z = place[0], place[1], place[2]

time: 71.6 us -> 71.5 us (level)
  no operation moved by 1% of the time
where the time goes in v5:
time: 71.5 us; the launch traced here: 71.4 us
  Pallas kernels  63.2 us (88%)
  local copies, waits for them, and re-layouts  7.39 us (10%)
  between operations  0.73 us (1%)
    pallas_call x1, Pallas kernels, per_device(): pl.pallas_call(kernel, out_shape=(block, block), in_specs=[vmem] * 7 + [h...  63.2 us
    unnamed x26, local copies, waits for them, and re-layouts  7.39 us

profile of v5, /device:TPU:1, one launch (start us, length us, event | category | flops | bytes accessed | tf_op | source)
XLA Modules:
  0.0 71.4 jit_solution(17753927551566272674)
XLA Ops:
  0.6 0.0 copy-start.9
  0.6 0.0 copy-start.7
  0.7 1.5 %copy.16.up_hbm = bf16[2,441,441]{2,1,0:T(8,128)(2,1)S(1)} copy(bf16[2,441,441]{2,0,1:T(2,128)(2,1)} %param.21) | data formatting | bytes 1555848 | tf_op args[9]
  2.1 0.0 copy-done.9
  2.1 1.1 %copy.17.tm_hbm = bf16[2,441,441]{2,1,0:T(8,128)(2,1)} copy(bf16[2,441,441]{2,0,1:T(2,128)(2,1)S(1)} %copy-done.9) | data formatting | bytes 1555848 | tf_op args[10]
  3.2 0.0 copy-done.7
  3.2 0.0 copy-start.8
  3.2 1.6 %copy.14.m2m_hbm = bf16[4,441,441]{2,1,0:T(8,128)(2,1)} copy(bf16[4,441,441]{2,0,1:T(4,128)(2,1)S(1)} %copy-done.7) | data formatting | bytes 3111696 | tf_op args[7]
  4.8 0.3 copy-done.8
  5.1 0.0 copy-start
  5.1 0.0 copy-start.1
  5.1 0.0 copy-start.2
  5.1 0.0 copy-start.3
  5.1 0.0 copy-start.4
  5.2 0.0 copy-start.5
  5.2 0.0 copy-start.6
  5.2 1.6 %copy.15.m2l_hbm = bf16[4,441,441]{2,1,0:T(8,128)(2,1)} copy(bf16[4,441,441]{2,0,1:T(4,128)(2,1)S(1)} %copy-done.8) | data formatting | bytes 3111696 | tf_op args[8]
  6.8 0.0 copy-done
  6.8 0.0 copy-done.1
  6.8 0.0 copy-done.2
  6.8 0.0 copy-done.3
  6.8 0.0 copy-done.4
  6.8 0.0 copy-done.5
  6.8 0.0 copy-done.6
  6.8 63.2 %vortex_wake.1 = (f32[3,64,128]{2,1,0:T(8,128)S(1)}, f32[3,64,128]{2,1,0:T(8,128)S(1)}) custom-call(f32[3,64,128]{2,1,0:T(8,128)S(1)} %bitcast.14, f32[3,64,128]{2,1,0:T(8,128)S(1)} %bitcast.15, s32[1,64]{1,0:T(1,128)S(1)} %copy-done.6, s32[1,256]{1,0:T(1,128)S(1)} %copy-done.4, s32[1,256]{1,0:T(1,128)S(1)} %copy-done.5, s32[16,64]{1,0:T(8,128)S(1)} %bitcast.18, ...), custom_call_target="tpu_custom_call" | custom-call | tf_op jit(solution)/shard_map/vortex_wake/pallas_call | solution.py:595
  70.1 0.6 copy.22
  70.7 0.6 copy.23
Async XLA Ops:
  0.6 1.5 %copy-start.9 = (bf16[2,441,441]{2,0,1:T(2,128)(2,1)S(1)}, bf16[2,441,441]{2,0,1:T(2,128)(2,1)}, u32[]{:S(2)}) copy-start(bf16[2,441,441]{2,0,1:T(2,128)(2,1)} %param.22) | copy-start | bytes 2333776
  0.6 2.6 %copy-start.7 = (bf16[4,441,441]{2,0,1:T(4,128)(2,1)S(1)}, bf16[4,441,441]{2,0,1:T(4,128)(2,1)}, u32[]{:S(2)}) copy-start(bf16[4,441,441]{2,0,1:T(4,128)(2,1)} %param.19) | copy-start | bytes 4667548
  3.2 1.9 %copy-start.8 = (bf16[4,441,441]{2,0,1:T(4,128)(2,1)S(1)}, bf16[4,441,441]{2,0,1:T(4,128)(2,1)}, u32[]{:S(2)}) copy-start(bf16[4,441,441]{2,0,1:T(4,128)(2,1)} %param.20) | copy-start | bytes 4667548
  5.1 1.6 %copy-start = (f32[3,1,64,128]{3,2,1,0:T(8,128)S(1)}, f32[3,1,64,128]{3,2,1,0:T(8,128)}, u32[]{:S(2)}) copy-start(f32[3,1,64,128]{3,2,1,0:T(8,128)} %param.12) | copy-start | bytes 294916
  5.1 1.6 %copy-start.1 = (f32[3,1,64,128]{3,2,1,0:T(8,128)S(1)}, f32[3,1,64,128]{3,2,1,0:T(8,128)}, u32[]{:S(2)}) copy-start(f32[3,1,64,128]{3,2,1,0:T(8,128)} %param.13) | copy-start | bytes 294916
  5.1 1.6 %copy-start.2 = (s32[1,64,16]{1,2,0:T(8,128)S(1)}, s32[1,64,16]{1,2,0:T(8,128)}, u32[]{:S(2)}) copy-start(s32[1,64,16]{1,2,0:T(8,128)} %param.17) | copy-start | bytes 12292
  5.1 1.6 %copy-start.3 = (s32[1,64,16]{1,2,0:T(8,128)S(1)}, s32[1,64,16]{1,2,0:T(8,128)}, u32[]{:S(2)}) copy-start(s32[1,64,16]{1,2,0:T(8,128)} %param.18) | copy-start | bytes 12292
  5.1 1.6 %copy-start.4 = (s32[1,256]{1,0:T(1,128)S(1)}, s32[1,256]{1,0:T(1,128)}, u32[]{:S(2)}) copy-start(s32[1,256]{1,0:T(1,128)} %cross_ref.1) | copy-start | bytes 3076
  5.2 1.6 %copy-start.5 = (s32[1,256]{1,0:T(1,128)S(1)}, s32[1,256]{1,0:T(1,128)}, u32[]{:S(2)}) copy-start(s32[1,256]{1,0:T(1,128)} %arr_ref.1) | copy-start | bytes 3076
  5.2 1.6 %copy-start.6 = (s32[1,64]{1,0:T(1,128)S(1)}, s32[1,64]{1,0:T(1,128)}, u32[]{:S(2)}) copy-start(s32[1,64]{1,0:T(1,128)} %cnt_ref.1) | copy-start | bytes 772
